TPU v7x, 32 devices: a whole 2x2x4 slice. The times are simulated.
32 devices in a mesh: gx: 4 (over y, core), gy: 8 (over z, x).
Axes of the slice: x: 2, y: 2, z: 4, core: 2. Of those that a mesh axis runs over, the one named last changes fastest.
Arguments:
- inputs: bfloat16 [1536, 7168], P('gy', 'gx'), may hold values from -6 to 6
- query_weight: bfloat16 [1792, 7168], P('gy', 'gx'), may hold values from -0.0625 to 0.0625
- key_weight: bfloat16 [1792, 7168], P('gy', 'gx'), may hold values from -0.0625 to 0.0625
- value_weight: bfloat16 [1792, 7168], P('gy', 'gx'), may hold values from -0.0625 to 0.0625
- adapter_down: bfloat16 [128, 7168], P(None, 'gx'), may hold values from -0.0625 to 0.0625
- adapter_up: bfloat16 [1792, 128], P('gy'), may hold values from -0.5 to 0.5
- prompt_keys: bfloat16 [4, 1792, 2048], P('gx', 'gy'), may hold values from -6 to 6
- prompt_values: bfloat16 [4, 1792, 2048], P('gx', 'gy'), may hold values from -6 to 6
- cache_keys: bfloat16 [32, 1792, 512], P('gx', 'gy'), may hold values from -240 to 240
- cache_values: bfloat16 [32, 1792, 512], P('gx', 'gy'), may hold values from -6 to 6
- cache_lengths: int32 [32], P('gx'), may hold values from 1 to 512, as said below
- parents: int32 [32, 48], P('gx'), may hold values from 0 to 46, as said below
- out_weight: bfloat16 [1792, 3584], P('gy', 'gx'), may hold values from -0.1875 to 0.1875
Outputs:
- layer_output: bfloat16 [1536, 3584], P('gx', 'gy')
Inputs may be any that keep to these rules, and one draw needn't show every extreme that they name: `parents`: node n's parent is a node below n, node 0 is its own parent, and node 47 hangs from node 46. `cache_lengths`: some request has all 512 positions valid.
All inputs are finite; a program needn't handle non-finite values.
Results may differ from a plain program's by a relative error of at most 0.017.
Values may be sent and summed in bfloat16 or wider, within the bound.
A program may use at most 128 MiB of HBM per device.

v0:
```python
import math

import jax
import jax.numpy as jnp
from jax import lax
from jax.sharding import PartitionSpec as P

HEAD = 224


def contract_rows(left, right):
    return lax.dot_general(
        left, right, (((1,), (1,)), ((), ())), preferred_element_type=jnp.float32
    )


def ancestors(parents):
    node_count = parents.shape[1]
    columns = jnp.arange(node_count, dtype=jnp.int32)
    parent_hot = (parents[:, :, None] == columns[None, None, :]).astype(jnp.float32)
    reached = jnp.minimum(jnp.eye(node_count, dtype=jnp.float32)[None] + parent_hot, 1.0)
    rounds = max(1, math.ceil(math.log2(node_count)))
    for sweep in range(rounds):
        reached = jnp.minimum(
            reached + jnp.einsum("rnm,rmk->rnk", reached, reached, precision=lax.Precision.HIGHEST),
            1.0,
        )
    return reached


def attend(queries, new_keys, new_values, prompt_k, prompt_v, cache_k, cache_v, lengths, parents):
    factor = 1.0 / math.sqrt(queries.shape[-1])
    s_prompt = (
        jnp.einsum("rnhe,hep->rnhp", queries, prompt_k, preferred_element_type=jnp.float32) * factor
    )
    s_cache = (
        jnp.einsum("rnhe,rhec->rnhc", queries, cache_k, preferred_element_type=jnp.float32) * factor
    )
    s_tree = (
        jnp.einsum("rnhe,rmhe->rnhm", queries, new_keys, preferred_element_type=jnp.float32)
        * factor
    )
    usable = jnp.arange(cache_k.shape[-1], dtype=jnp.int32)[None, :] < lengths[:, None]
    s_cache = jnp.where(usable[:, None, None, :], s_cache, -jnp.inf)
    reached = ancestors(parents)
    s_tree = jnp.where(reached[:, :, None, :] > 0.5, s_tree, -jnp.inf)
    largest = jnp.maximum(
        jnp.maximum(
            jnp.max(s_prompt, axis=-1, keepdims=True), jnp.max(s_cache, axis=-1, keepdims=True)
        ),
        jnp.max(s_tree, axis=-1, keepdims=True),
    )
    e_prompt = jnp.exp(s_prompt - largest)
    e_cache = jnp.exp(s_cache - largest)
    e_tree = jnp.exp(s_tree - largest)
    totals = (
        jnp.sum(e_prompt, axis=-1, keepdims=True)
        + jnp.sum(e_cache, axis=-1, keepdims=True)
        + jnp.sum(e_tree, axis=-1, keepdims=True)
    )
    w_prompt = (e_prompt / totals).astype(jnp.bfloat16)
    w_cache = (e_cache / totals).astype(jnp.bfloat16)
    w_tree = (e_tree / totals).astype(jnp.bfloat16)
    result = jnp.einsum("rnhp,hep->rnhe", w_prompt, prompt_v, preferred_element_type=jnp.float32)
    result = result + jnp.einsum(
        "rnhc,rhec->rnhe", w_cache, cache_v, preferred_element_type=jnp.float32
    )
    result = result + jnp.einsum(
        "rnhm,rmhe->rnhe", w_tree, new_values, preferred_element_type=jnp.float32
    )
    return result.astype(jnp.bfloat16)


def per_device(
    inputs,
    query_weight,
    key_weight,
    value_weight,
    adapter_down,
    adapter_up,
    prompt_keys,
    prompt_values,
    cache_keys,
    cache_values,
    cache_lengths,
    parents,
    out_weight,
):
    requests = cache_keys.shape[0]
    node_count = parents.shape[1]
    local_rows = requests * node_count
    head_width = query_weight.shape[0]
    all_rows = lax.all_gather(inputs, "gy", axis=0, tiled=True)
    mixture = lax.psum_scatter(
        jnp.concatenate(
            [
                contract_rows(all_rows, matrix)
                for matrix in (query_weight, key_weight, value_weight, adapter_down)
            ],
            axis=1,
        ),
        "gx",
        scatter_dimension=0,
        tiled=True,
    )
    head_count = head_width // HEAD
    query_base = mixture[:, :head_width]
    new_keys = mixture[:, head_width : 2 * head_width].astype(jnp.bfloat16)
    new_values = mixture[:, 2 * head_width : 3 * head_width].astype(jnp.bfloat16)
    adapter_mid = mixture[:, 3 * head_width :].astype(jnp.bfloat16)
    queries = (query_base + contract_rows(adapter_mid, adapter_up)).astype(jnp.bfloat16)
    shaped = (requests, node_count, head_count, HEAD)
    cached = (requests, head_count, HEAD, cache_keys.shape[2])
    attended = attend(
        queries.reshape(shaped),
        new_keys.reshape(shaped),
        new_values.reshape(shaped),
        prompt_keys,
        prompt_values,
        cache_keys.reshape(cached),
        cache_values.reshape(cached),
        cache_lengths,
        parents,
    )
    flattened = attended.reshape(local_rows, head_width)
    partial_sums = jnp.dot(
        flattened,
        lax.all_gather(out_weight, "gx", axis=1, tiled=True),
        preferred_element_type=jnp.float32,
    )
    return lax.psum_scatter(
        partial_sums.astype(jnp.bfloat16), "gy", scatter_dimension=1, tiled=True
    )


def solution(mesh):
    placed = (
        P("gy", "gx"),
        P("gy", "gx"),
        P("gy", "gx"),
        P("gy", "gx"),
        P(None, "gx"),
        P("gy", None),
        P("gx", "gy", None),
        P("gx", "gy", None),
        P("gx", "gy", None),
        P("gx", "gy", None),
        P("gx"),
        P("gx", None),
        P("gy", "gx"),
    )
    return jax.shard_map(
        per_device, mesh=mesh, in_specs=placed, out_specs=P("gx", "gy"), check_vma=False
    )
```

profile of v0, /device:TPU:0, one launch (start us, length us, event | category | flops | bytes accessed | tf_op | source)
XLA Modules:
  0.0 265.4 jit_solution(2232846366430810138)
XLA Ops:
  6.5 0.7 all-gather.3.cloned.1.call-update
  7.3 94.4 %all-gather.3.cloned.1.call-done = bf16[1536,1792]{1,0:T(8,128)(2,1)} async-done(((bf16[192,1792]{1,0:T(8,128)(2,1)}), bf16[1536,1792]{1,0:T(8,128)(2,1)}) %all-gather.3.cloned.1.call-update) | async-done | bytes 5505040 | tf_op jit(solution)/shard_map/all_gather | solution.py:93
  101.7 4.7 %fusion.44 = f32[1536,224]{0,1:T(8,128)S(1)} fusion(bf16[1536,1792]{1,0:T(8,128)(2,1)} %all-gather.3.cloned.1.call-done, bf16[224,1792]{1,0:T(8,128)(2,1)} %param.14), kind=kOutput, calls=%fused_computation.68 | convolution fusion | flops 1233125376 | bytes 7684096 | tf_op jit(solution)/shard_map/dot_general | solution.py:12
  106.4 1.8 fusion.45
  108.2 1.7 fusion.46
  110.0 1.9 fusion.47
  111.8 2.5 pad_maximum_fusion
  114.5 0.7 all-gather.5.cloned.1.call-update
  115.2 0.4 fusion.14
  115.6 0.3 fusion.15
  115.9 0.3 fusion.16
  116.2 0.3 fusion.17
  116.5 0.3 fusion.18
  116.8 0.3 fusion.23
  117.3 44.7 %reduce-scatter.3.cloned.1.call-done = f32[384,800]{0,1:T(8,128)} async-done(((f32[1536,800]{0,1:T(8,128)}), f32[384,800]{0,1:T(8,128)}) %reduce-scatter.3.cloned.1.call-update) | async-done | bytes 1228816 | tf_op jit(solution)/shard_map/reduce_scatter | solution.py:94
  162.0 1.4 convert.5
  163.4 1.2 fusion.13
  164.6 0.1 copy.26
  164.7 0.1 copy.33
  164.9 0.5 fusion.43
  165.4 0.2 fusion.42
  165.6 0.1 copy.34
  165.8 1.8 bitcast_reduce_fusion
  167.7 0.3 fusion.26
  168.0 0.6 fusion.1
  168.5 0.3 convolution_bitcast_fusion
  168.8 0.7 fusion.7
  169.6 0.8 copy-done.5
  170.4 0.7 fusion.12
  171.1 12.4 %all-gather.5.cloned.1.call-done = bf16[224,3584]{1,0:T(8,128)(2,1)} async-done(((bf16[224,896]{1,0:T(8,128)(2,1)}), bf16[224,3584]{1,0:T(8,128)(2,1)}) %all-gather.5.cloned.1.call-update) | async-done | bytes 1605648 | tf_op jit(solution)/shard_map/all_gather | solution.py:128
  183.5 4.2 %convolution_convert_fusion = bf16[384,3584]{0,1:T(8,128)(2,1)} fusion(bf16[384,224]{1,0:T(8,128)(2,1)S(1)} %bitcast.115, bf16[224,3584]{1,0:T(8,128)(2,1)} %all-gather.5.cloned.1.call-done), kind=kOutput, calls=%fused_computation | convolution fusion | flops 617938944 | bytes 4530176 | tf_op jit(solution)/shard_map/dot_general | solution.py:126
  187.7 71.1 %reduce-scatter.5.cloned.1.call-done = bf16[384,448]{0,1:T(8,128)(2,1)} async-done(((bf16[384,3584]{0,1:T(8,128)(2,1)}), bf16[384,448]{0,1:T(8,128)(2,1)}) %reduce-scatter.5.cloned.1.call-update) | async-done | bytes 344080 | tf_op jit(solution)/shard_map/reduce_scatter | solution.py:131
  (31 shorter events, 0.4 us)
Async XLA Ops:
  6.5 158.3 %copy-start = (bf16[8,224,512]{2,1,0:T(8,128)(2,1)S(1)}, bf16[8,224,512]{2,1,0:T(8,128)(2,1)}, u32[]{:S(2)}) copy-start(bf16[8,224,512]{2,1,0:T(8,128)(2,1)} %param.21) | copy-start | bytes 5505028
  6.5 95.2 %all-gather.3.cloned.1.call-start = ((), (), s32[]{:S(2)}) async-start(), calls=%async_computation.2 | async-start | bytes 6193152 | tf_op jit(solution)/shard_map/all_gather | solution.py:93
  7.3 99.1 %copy-start.7 = (bf16[224,1792]{1,0:T(8,128)(2,1)S(1)}, bf16[224,1792]{1,0:T(8,128)(2,1)}, u32[]{:S(2)}) copy-start(bf16[224,1792]{1,0:T(8,128)(2,1)} %param.15) | copy-start | bytes 2408452
  7.3 154.7 %reduce-scatter.3.cloned.1.call-start = ((), (), s32[]{:S(2)}) async-start(), calls=%async_computation.3 | async-start | bytes 6144000 | tf_op jit(solution)/shard_map/reduce_scatter | solution.py:94
  101.7 4.7 %copy-start.1 = (bf16[1536,1792]{1,0:T(8,128)(2,1)S(1)}, bf16[1536,1792]{1,0:T(8,128)(2,1)}, u32[]{:S(2)}) copy-start(bf16[1536,1792]{1,0:T(8,128)(2,1)} %all-gather.3.cloned.1.call-done) | copy-start | bytes 16515076
  106.4 1.8 copy-start.8
  108.2 1.8 copy-start.2
  114.4 0.8 copy-start.9
  114.4 2.8 %copy-start.4 = (s32[8]{0:T(128)S(1)}, s32[8]{0:T(128)}, u32[]{:S(2)}) copy-start(s32[8]{0:T(128)} %param.23) | copy-start | bytes 100
  114.4 49.0 %copy-start.3 = (bf16[224,128]{1,0:T(8,128)(2,1)S(1)}, bf16[224,128]{1,0:T(8,128)(2,1)}, u32[]{:S(2)}) copy-start(bf16[224,128]{1,0:T(8,128)(2,1)} %param.18) | copy-start | bytes 172036
  114.4 69.1 %all-gather.5.cloned.1.call-start = ((), (), s32[]{:S(2)}) async-start(), calls=%async_computation.4 | async-start | bytes 2007040 | tf_op jit(solution)/shard_map/all_gather | solution.py:128
  115.1 143.7 %reduce-scatter.5.cloned.1.call-start = ((), (), s32[]{:S(2)}) async-start(), calls=%async_computation.5 | async-start | bytes 3096576 | tf_op jit(solution)/shard_map/reduce_scatter | solution.py:131
  167.6 1.2 copy-start.6
  168.8 1.6 copy-start.5
Sparse Core Ops, SparseCore 0:
  9.5 92.1 all-gather.2
  114.5 47.4 reduce-scatter.2
  163.6 19.8 all-gather.4
  187.9 70.9 reduce-scatter.4
where the time goes:
time: 266 us; the launch traced here: 265 us
  waiting for transfers between devices  224 us (84%)
  matrix products  21.6 us (8%)
  between operations  13.4 us (5%)
  other arithmetic  4.83 us (2%)
    all_gather x1, waiting for transfers between devices, per_device(): all_rows = lax.all_gather(inputs, 'gy', axis=0, tiled=True)  94.4 us
    reduce_scatter x1, waiting for transfers between devices, per_device(): lax.psum_scatter(partial_sums.astype(jnp.bfloat16), 'gy', scatter_dimensi...  71.1 us
    reduce_scatter x1, waiting for transfers between devices, per_device(): lax.psum_scatter(jnp.concatenate([contract_rows(all_rows, matrix) for mat...  44.7 us
    all_gather x1, waiting for transfers between devices, per_device(): lax.all_gather(out_weight, 'gx', axis=1, tiled=True)  12.4 us
    dot_general x5, matrix products, contract_rows(): lax.dot_general(left, right, (((1,), (1,)), ((), ())), preferred_element_...  11.2 us
  transfers between devices with their start and end apart: 4, of which 4 were waited for; matrix products, arithmetic and copies ran while one was open for 4% of the time, Pallas kernels for 0%

commit v1 on v0

--- a/solution.py
+++ b/solution.py
@@ -3,15 +3,17 @@
 import jax
 import jax.numpy as jnp
 from jax import lax
+from jax.experimental import pallas as pl
+from jax.experimental.pallas import tpu as pltpu
 from jax.sharding import PartitionSpec as P
 
 HEAD = 224
+NT = (((1,), (1,)), ((), ()))
+MESH = pl.DeviceIdType.MESH
 
 
 def contract_rows(left, right):
-    return lax.dot_general(
-        left, right, (((1,), (1,)), ((), ())), preferred_element_type=jnp.float32
-    )
+    return lax.dot_general(left, right, NT, preferred_element_type=jnp.float32)
 
 
 def ancestors(parents):
@@ -19,16 +21,15 @@
     columns = jnp.arange(node_count, dtype=jnp.int32)
     parent_hot = (parents[:, :, None] == columns[None, None, :]).astype(jnp.float32)
     reached = jnp.minimum(jnp.eye(node_count, dtype=jnp.float32)[None] + parent_hot, 1.0)
+    reached = reached.astype(jnp.bfloat16)
     rounds = max(1, math.ceil(math.log2(node_count)))
     for sweep in range(rounds):
-        reached = jnp.minimum(
-            reached + jnp.einsum("rnm,rmk->rnk", reached, reached, precision=lax.Precision.HIGHEST),
-            1.0,
-        )
+        step = jnp.einsum("rnm,rmk->rnk", reached, reached, preferred_element_type=jnp.float32)
+        reached = jnp.minimum(reached.astype(jnp.float32) + step, 1.0).astype(jnp.bfloat16)
     return reached
 
 
-def attend(queries, new_keys, new_values, prompt_k, prompt_v, cache_k, cache_v, lengths, parents):
+def attend(queries, new_keys, new_values, prompt_k, prompt_v, cache_k, cache_v, lengths, reached):
     factor = 1.0 / math.sqrt(queries.shape[-1])
     s_prompt = (
         jnp.einsum("rnhe,hep->rnhp", queries, prompt_k, preferred_element_type=jnp.float32) * factor
@@ -42,7 +43,6 @@
     )
     usable = jnp.arange(cache_k.shape[-1], dtype=jnp.int32)[None, :] < lengths[:, None]
     s_cache = jnp.where(usable[:, None, None, :], s_cache, -jnp.inf)
-    reached = ancestors(parents)
     s_tree = jnp.where(reached[:, :, None, :] > 0.5, s_tree, -jnp.inf)
     largest = jnp.maximum(
         jnp.maximum(
@@ -69,6 +69,461 @@
         "rnhm,rmhe->rnhe", w_tree, new_values, preferred_element_type=jnp.float32
     )
     return result.astype(jnp.bfloat16)
+
+
+def remote(src, dst, send, recv, axis, index):
+    return pltpu.make_async_remote_copy(
+        src_ref=src,
+        dst_ref=dst,
+        send_sem=send,
+        recv_sem=recv,
+        device_id={axis: index},
+        device_id_type=MESH,
+    )
+
+
+def line_position():
+    h = lax.axis_index("gy")
+    z = h // 2
+    x = h - 2 * z
+    return z, x
+
+
+def greet_line(planes, z, x, extra):
+    barrier = pltpu.get_barrier_semaphore()
+
+    def signal(axis, index):
+        pl.semaphore_signal(barrier, inc=1, device_id={axis: index}, device_id_type=MESH)
+
+    signal("gy", 2 * z + 1 - x)
+    for index in extra:
+        signal("gx", index)
+
+    @pl.when(z > 0)
+    def _():
+        signal("gy", 2 * (z - 1) + x)
+
+    @pl.when(z < planes - 1)
+    def _():
+        signal("gy", 2 * (z + 1) + x)
+
+    inner = jnp.where(z > 0, 1, 0) + jnp.where(z < planes - 1, 1, 0)
+    pl.semaphore_wait(barrier, 1 + len(extra) + inner)
+
+
+def pieces_of(rows):
+    late = rows // 6
+    half = (rows - late) // 2
+    return ((0, half), (half, half), (2 * half, late))
+
+
+def project_kernel(
+    planes,
+    x_ref,
+    wq,
+    wk,
+    wv,
+    wd,
+    up,
+    out,
+    rows_buf,
+    weights,
+    part,
+    core_in,
+    y_out,
+    y_in,
+    w_sem,
+    up_send,
+    down_send,
+    x_send,
+    recv,
+    c_send,
+    c_recv,
+    y_send,
+    y_recv,
+):
+    z, x = line_position()
+    mine = lax.axis_index("gx")
+    y = mine // 2
+    core = mine - 2 * y
+    other_core = 2 * y + 1 - core
+    other_y = 2 * (1 - y) + core
+    shard = x_ref.shape[0]
+    group_rows = 2 * shard
+    ranges = pieces_of(shard)
+    width = wq.shape[0]
+
+    loads = []
+    start = 0
+    for slot, matrix in enumerate((wq, wk, wv, wd)):
+        count = matrix.shape[0]
+        load = pltpu.make_async_copy(
+            matrix, weights.at[pl.ds(start, count)], w_sem.at[slot]
+        )
+        load.start()
+        loads.append(load)
+        start += count
+    greet_line(planes, z, x, (other_core, other_y))
+
+    def place(oz, ox, p):
+        first, count = ranges[p]
+        return rows_buf.at[pl.ds(pl.multiple_of((2 * oz + ox) * shard + first, 16), count)]
+
+    def own(p):
+        first, count = ranges[p]
+        return x_ref.at[pl.ds(first, count)]
+
+    def to_x(oz, ox, p, src):
+        return remote(
+            src, place(oz, ox, p), x_send.at[oz, p], recv.at[2 * oz + ox, p], "gy", 2 * z + 1 - x
+        )
+
+    def to_up(oz, ox, p, src):
+        return remote(
+            src,
+            place(oz, ox, p),
+            up_send.at[2 * oz + ox, p],
+            recv.at[2 * oz + ox, p],
+            "gy",
+            2 * jnp.minimum(z + 1, planes - 1) + x,
+        )
+
+    def to_down(oz, ox, p, src):
+        return remote(
+            src,
+            place(oz, ox, p),
+            down_send.at[2 * oz + ox, p],
+            recv.at[2 * oz + ox, p],
+            "gy",
+            2 * jnp.maximum(z - 1, 0) + x,
+        )
+
+    def arrived(oz, ox, p):
+        ref = place(oz, ox, p)
+        remote(ref, ref, x_send.at[0, 0], recv.at[2 * oz + ox, p], "gy", 2 * z + 1 - x).wait_recv()
+
+    def both_ways(oz, ox, p, src):
+        @pl.when(z < planes - 1)
+        def _():
+            to_up(oz, ox, p, src).start()
+
+        @pl.when(z > 0)
+        def _():
+            to_down(oz, ox, p, src).start()
+
+    to_x(z, x, 2, own(2)).start()
+    for p in (0, 1, 2):
+        both_ways(z, x, p, own(p))
+        if p < 2:
+            to_x(z, x, p, own(p)).start()
+    rows_buf[pl.ds(pl.multiple_of((2 * z + x) * shard, 16), shard)] = x_ref[...]
+    arrived(z, 1 - x, 2)
+    both_ways(z, 1 - x, 2, place(z, 1 - x, 2))
+    for load in loads:
+        load.wait()
+
+    def from_side(oz, below, p, ox):
+        @pl.when(jnp.logical_and(oz >= 0, oz < planes))
+        def _():
+            arrived(oz, ox, p)
+            src = place(oz, ox, p)
+            if below:
+
+                @pl.when(z < planes - 1)
+                def _():
+                    to_up(oz, ox, p, src).start()
+            else:
+
+                @pl.when(z > 0)
+                def _():
+                    to_down(oz, ox, p, src).start()
+
+    def from_sides(distance, p, ox, cross):
+        for below in (True, False):
+            oz = z - distance if below else z + distance
+            from_side(oz, below, p, ox)
+            if cross:
+
+                @pl.when(jnp.logical_and(oz >= 0, oz < planes))
+                def _():
+                    to_x(oz, x, p, place(oz, x, p)).start()
+
+    def group_at(k):
+        last = planes - 1
+        low = jnp.where(z == 0, k, jnp.where(k == 0, 1, jnp.where(k == 1, 0, k)))
+        m = last - z
+        high = jnp.where(m == 0, k, jnp.where(k == 0, 1, jnp.where(k == 1, 0, k)))
+        return jnp.where(z < 2, low, last - high)
+
+    def core_copy(g):
+        return remote(
+            part.at[g], core_in.at[g // 2], c_send.at[g // 2], c_recv.at[g // 2], "gx", other_core
+        )
+
+    def y_copy():
+        return remote(y_out, y_in, y_send.at[0], y_recv.at[0], "gx", other_y)
+
+    def settle(g):
+        @pl.when(g - 2 * (g // 2) == core)
+        def _():
+            core_copy(g).wait_recv()
+
+            @pl.when(g // 2 != y)
+            def _():
+                y_out[...] = (part[g] + core_in[g // 2]).astype(y_out.dtype)
+                y_copy().start()
+
+    def step(k, carry):
+        distance = k + 1
+        for p in (0, 1):
+            from_sides(distance, p, x, True)
+        for ox in (x, 1 - x):
+            from_sides(distance, 2, ox, False)
+
+        @pl.when(k > 0)
+        def _():
+            settle(group_at(k - 1))
+
+        g = group_at(k)
+        for p in (0, 1):
+            arrived(g, 1 - x, p)
+        part[g] = lax.dot_general(
+            weights[...],
+            rows_buf[pl.ds(pl.multiple_of(g * group_rows, 16), group_rows)],
+            NT,
+            preferred_element_type=jnp.float32,
+        )
+
+        @pl.when(g - 2 * (g // 2) != core)
+        def _():
+            core_copy(g).start()
+
+        return carry
+
+    lax.fori_loop(0, planes, step, 0)
+    settle(group_at(planes - 1))
+    y_copy().wait_recv()
+    total = part[mine] + core_in[mine // 2] + y_in[...].astype(jnp.float32)
+    middle = total[3 * width :].astype(jnp.bfloat16)
+    extra = jnp.dot(up[...], middle, preferred_element_type=jnp.float32)
+    out[pl.ds(0, width)] = (total[:width] + extra).astype(jnp.bfloat16)
+    out[pl.ds(width, 2 * width)] = total[width : 3 * width].astype(jnp.bfloat16)
+
+    y_copy().wait_send()
+    for half in range(planes // 2):
+        core_copy(2 * half + 1 - core).wait_send()
+    for oz in range(planes):
+        for p in (0, 1):
+            to_x(oz, x, p, place(oz, x, p)).wait_send()
+        for ox in (0, 1):
+            for p in (0, 1, 2):
+                if p == 2:
+                    sent = oz >= 0
+                else:
+                    sent = x == ox
+
+                @pl.when(jnp.logical_and(sent, jnp.logical_and(oz <= z, z < planes - 1)))
+                def _():
+                    to_up(oz, ox, p, place(oz, ox, p)).wait_send()
+
+                @pl.when(jnp.logical_and(sent, jnp.logical_and(oz >= z, z > 0)))
+                def _():
+                    to_down(oz, ox, p, place(oz, ox, p)).wait_send()
+
+    to_x(z, x, 2, own(2)).wait_send()
+
+
+def project(inputs, query_weight, key_weight, value_weight, adapter_down, adapter_up, planes):
+    shard, columns = inputs.shape
+    features = 3 * query_weight.shape[0] + adapter_down.shape[0]
+    tokens = 2 * shard
+    dma = pltpu.SemaphoreType.DMA
+    vmem = pl.BlockSpec(memory_space=pltpu.VMEM)
+    anywhere = pl.BlockSpec(memory_space=pl.ANY)
+
+    def kernel(*refs):
+        project_kernel(planes, *refs)
+
+    return pl.pallas_call(
+        kernel,
+        out_shape=jax.ShapeDtypeStruct((3 * query_weight.shape[0], tokens), jnp.bfloat16),
+        in_specs=[vmem, anywhere, anywhere, anywhere, anywhere, vmem],
+        out_specs=vmem,
+        scratch_shapes=[
+            pltpu.VMEM((planes * tokens, columns), jnp.bfloat16),
+            pltpu.VMEM((features, columns), jnp.bfloat16),
+            pltpu.VMEM((planes, features, tokens), jnp.float32),
+            pltpu.VMEM((planes // 2, features, tokens), jnp.float32),
+            pltpu.VMEM((features, tokens), jnp.bfloat16),
+            pltpu.VMEM((features, tokens), jnp.bfloat16),
+            dma((4,)),
+            dma((2 * planes, 3)),
+            dma((2 * planes, 3)),
+            dma((planes, 3)),
+            dma((2 * planes, 3)),
+            dma((planes // 2,)),
+            dma((planes // 2,)),
+            dma((1,)),
+            dma((1,)),
+        ],
+        compiler_params=pltpu.CompilerParams(
+            collective_id=0, has_side_effects=True, vmem_limit_bytes=44 * 1024 * 1024
+        ),
+        cost_estimate=pl.CostEstimate(
+            flops=2 * planes * tokens * columns * features,
+            bytes_accessed=2 * (planes * tokens + features) * columns,
+            transcendentals=0,
+        ),
+    )(inputs, query_weight, key_weight, value_weight, adapter_down, adapter_up)
+
+
+def output_kernel(
+    planes,
+    att,
+    weight,
+    out,
+    x_out,
+    x_in,
+    kept,
+    z_out,
+    up_in,
+    down_in,
+    x_send,
+    x_recv,
+    z_send,
+    up_recv,
+    down_recv,
+):
+    z, x = line_position()
+    block = out.shape[0]
+    greet_line(planes, z, x, ())
+
+    def partial(oz, ox):
+        rows = weight[pl.ds(pl.multiple_of((2 * oz + ox) * block, 16), block)]
+        return lax.dot_general(rows, att[...], NT, preferred_element_type=jnp.float32)
+
+    def plane_at(k):
+        last = planes - 1
+        low = jnp.where(z == 0, last - k, jnp.where(k == 0, 3, jnp.where(k == 1, 0, 3 - k + 1)))
+        low = jnp.where(jnp.logical_and(z == 1, k == 3), 1, low)
+        m = last - z
+        high = jnp.where(m == 0, last - k, jnp.where(k == 0, 3, jnp.where(k == 1, 0, 3 - k + 1)))
+        high = jnp.where(jnp.logical_and(m == 1, k == 3), 1, high)
+        return jnp.where(z < 2, low, last - high)
+
+    def x_copy(oz):
+        return remote(
+            x_out.at[oz], x_in.at[oz], x_send.at[oz], x_recv.at[oz], "gy", 2 * z + 1 - x
+        )
+
+    def up_copy(oz):
+        return remote(
+            z_out.at[oz],
+            up_in.at[oz],
+            z_send.at[oz],
+            up_recv.at[oz],
+            "gy",
+            2 * jnp.minimum(z + 1, planes - 1) + x,
+        )
+
+    def down_copy(oz):
+        return remote(
+            z_out.at[oz],
+            down_in.at[oz],
+            z_send.at[oz],
+            down_recv.at[oz],
+            "gy",
+            2 * jnp.maximum(z - 1, 0) + x,
+        )
+
+    def cross(k, carry):
+        oz = plane_at(k)
+        x_out[oz] = partial(oz, 1 - x).astype(x_out.dtype)
+        x_copy(oz).start()
+        return carry
+
+    lax.fori_loop(0, planes, cross, 0)
+
+    def keep(k, carry):
+        kept[k] = partial(k, x)
+        return carry
+
+    lax.fori_loop(0, planes, keep, 0)
+
+    def along(k, carry):
+        oz = plane_at(k)
+        x_copy(oz).wait_recv()
+        kept[oz] = kept[oz] + x_in[oz].astype(jnp.float32)
+
+        @pl.when(jnp.logical_and(z > 0, oz >= z))
+        def _():
+            up_copy(oz).wait_recv()
+            kept[oz] = kept[oz] + up_in[oz].astype(jnp.float32)
+
+        @pl.when(jnp.logical_and(z < planes - 1, oz <= z))
+        def _():
+            down_copy(oz).wait_recv()
+            kept[oz] = kept[oz] + down_in[oz].astype(jnp.float32)
+
+        @pl.when(oz > z)
+        def _():
+            z_out[oz] = kept[oz].astype(z_out.dtype)
+            up_copy(oz).start()
+
+        @pl.when(oz < z)
+        def _():
+            z_out[oz] = kept[oz].astype(z_out.dtype)
+            down_copy(oz).start()
+
+        return carry
+
+    lax.fori_loop(0, planes, along, 0)
+    out[...] = kept[z].astype(out.dtype)
+
+    def finish(oz, carry):
+        x_copy(oz).wait_send()
+
+        @pl.when(oz != z)
+        def _():
+            up_copy(oz).wait_send()
+
+        return carry
+
+    lax.fori_loop(0, planes, finish, 0)
+
+
+def project_out(att, weight, planes):
+    tokens = att.shape[0]
+    block = weight.shape[0] // (2 * planes)
+    dma = pltpu.SemaphoreType.DMA
+    vmem = pl.BlockSpec(memory_space=pltpu.VMEM)
+    blocks = (planes, block, tokens)
+
+    def kernel(*refs):
+        output_kernel(planes, *refs)
+
+    return pl.pallas_call(
+        kernel,
+        out_shape=jax.ShapeDtypeStruct((block, tokens), jnp.bfloat16),
+        in_specs=[vmem, vmem],
+        out_specs=vmem,
+        scratch_shapes=[
+            pltpu.VMEM(blocks, jnp.bfloat16),
+            pltpu.VMEM(blocks, jnp.bfloat16),
+            pltpu.VMEM(blocks, jnp.float32),
+            pltpu.VMEM(blocks, jnp.bfloat16),
+            pltpu.VMEM(blocks, jnp.bfloat16),
+            pltpu.VMEM(blocks, jnp.bfloat16),
+            dma((planes,)),
+            dma((planes,)),
+            dma((planes,)),
+            dma((planes,)),
+            dma((planes,)),
+        ],
+        compiler_params=pltpu.CompilerParams(
+            collective_id=1, has_side_effects=True, vmem_limit_bytes=32 * 1024 * 1024
+        ),
+    )(att, weight)
 
 
 def per_device(
@@ -90,27 +545,39 @@
     node_count = parents.shape[1]
     local_rows = requests * node_count
     head_width = query_weight.shape[0]
-    all_rows = lax.all_gather(inputs, "gy", axis=0, tiled=True)
-    mixture = lax.psum_scatter(
-        jnp.concatenate(
-            [
-                contract_rows(all_rows, matrix)
-                for matrix in (query_weight, key_weight, value_weight, adapter_down)
-            ],
-            axis=1,
-        ),
-        "gx",
-        scatter_dimension=0,
-        tiled=True,
-    )
     head_count = head_width // HEAD
-    query_base = mixture[:, :head_width]
-    new_keys = mixture[:, head_width : 2 * head_width].astype(jnp.bfloat16)
-    new_values = mixture[:, 2 * head_width : 3 * head_width].astype(jnp.bfloat16)
-    adapter_mid = mixture[:, 3 * head_width :].astype(jnp.bfloat16)
-    queries = (query_base + contract_rows(adapter_mid, adapter_up)).astype(jnp.bfloat16)
+    lines = lax.axis_size("gx") == 4 and lax.axis_size("gy") == 8
     shaped = (requests, node_count, head_count, HEAD)
     cached = (requests, head_count, HEAD, cache_keys.shape[2])
+    reached = ancestors(parents)
+    if lines:
+        planes = lax.axis_size("gy") // 2
+        gathered_weight = lax.all_gather(out_weight.T, "gx", axis=0, tiled=True)
+        projected = project(
+            inputs, query_weight, key_weight, value_weight, adapter_down, adapter_up, planes
+        )
+        queries = projected[:head_width].T
+        new_keys = projected[head_width : 2 * head_width].T
+        new_values = projected[2 * head_width :].T
+    else:
+        all_rows = lax.all_gather(inputs, "gy", axis=0, tiled=True)
+        mixture = lax.psum_scatter(
+            jnp.concatenate(
+                [
+                    contract_rows(all_rows, matrix)
+                    for matrix in (query_weight, key_weight, value_weight, adapter_down)
+                ],
+                axis=1,
+            ),
+            "gx",
+            scatter_dimension=0,
+            tiled=True,
+        )
+        query_base = mixture[:, :head_width]
+        new_keys = mixture[:, head_width : 2 * head_width].astype(jnp.bfloat16)
+        new_values = mixture[:, 2 * head_width : 3 * head_width].astype(jnp.bfloat16)
+        adapter_mid = mixture[:, 3 * head_width :].astype(jnp.bfloat16)
+        queries = (query_base + contract_rows(adapter_mid, adapter_up)).astype(jnp.bfloat16)
     attended = attend(
         queries.reshape(shaped),
         new_keys.reshape(shaped),
@@ -120,9 +587,11 @@
         cache_keys.reshape(cached),
         cache_values.reshape(cached),
         cache_lengths,
-        parents,
+        reached,
     )
     flattened = attended.reshape(local_rows, head_width)
+    if lines:
+        return project_out(flattened, gathered_weight, planes).T
     partial_sums = jnp.dot(
         flattened,
         lax.all_gather(out_weight, "gx", axis=1, tiled=True),

time: 266 us -> 146 us (0.55)
  waiting for transfers between devices: 224 us -> 0.04 us
  Pallas kernels: 0 us -> 113 us
  matrix products: 21.6 us -> 5.44 us
  local copies, waits for them, and re-layouts: 1.35 us -> 11.9 us
  other arithmetic: 4.83 us -> 0.96 us
    reduce_scatter x2 -> x0, waiting for transfers between devices: 116 us -> none  [the longest x1 71.1 us: per_device(): lax.psum_scatter(partial_sums.astype(jnp.bfloat16), 'gy', scatter_dimensi...]
    pallas_call x0 -> x2, Pallas kernels: none -> 113 us  [the longest x1 71.3 us: project(): pl.pallas_call(kernel, out_shape=jax.ShapeDtypeStruct((3 * query_weight.s...]
    all_gather x2 -> x1, waiting for transfers between devices: 107 us -> 0.02 us  [per_device(): gathered_weight = lax.all_gather(out_weight.T, 'gx', axis=0, tiled=True)]
    dot_general x12 -> x6, matrix products: 17.3 us -> 1.13 us  [ancestors(): jnp.einsum('rnm,rmk->rnk', reached, reached, preferred_element_type=jnp.f...]
    unnamed x20 -> x26, local copies, waits for them, and re-layouts: 0.88 us -> 11.5 us
  transfers between devices with their start and end apart: 4 -> 1, of which waited for: 4 -> 0; matrix products, arithmetic and copies ran while one was open for 4% -> 5% of each run, Pallas kernels for 0% -> 49%
where the time goes in v1:
time: 146 us; the launch traced here: 145 us
  Pallas kernels  113 us (77%)
  between operations  13.6 us (9%)
  local copies, waits for them, and re-layouts  11.9 us (8%)
  matrix products  5.44 us (4%)
    pallas_call x1, Pallas kernels, project(): pl.pallas_call(kernel, out_shape=jax.ShapeDtypeStruct((3 * query_weight.s...  71.3 us
    pallas_call x1, Pallas kernels, project_out(): pl.pallas_call(kernel, out_shape=jax.ShapeDtypeStruct((block, tokens), jn...  42.1 us
    unnamed x26, local copies, waits for them, and re-layouts  11.5 us
  transfers between devices with their start and end apart: 1, of which 0 were waited for; matrix products, arithmetic and copies ran while one was open for 5% of the time, Pallas kernels for 49%

profile of v1, /device:TPU:0, one launch (start us, length us, event | category | flops | bytes accessed | tf_op | source)
XLA Modules:
  0.0 145.5 jit_solution(6210953047447965616)
XLA Ops:
  6.5 2.1 %copy.37 = bf16[224,896]{0,1:T(8,128)(2,1)} copy(bf16[224,896]{1,0:T(8,128)(2,1)} %param.25) | data formatting | bytes 802816 | tf_op args[12]
  8.7 1.1 copy-done.2
  9.8 1.1 copy-done.3
  11.0 1.1 copy-done.4
  12.1 1.1 copy-done.5
  13.2 1.0 copy-done.6
  14.2 0.8 copy-done.7
  15.1 71.3 %shard_map.127 = bf16[672,384]{1,0:T(8,128)(2,1)S(1)} custom-call(bf16[192,1792]{1,0:T(8,128)(2,1)S(1)} %copy-done.5, bf16[224,1792]{1,0:T(8,128)(2,1)S(1)} %copy-done.2, bf16[224,1792]{1,0:T(8,128)(2,1)S(1)} %copy-done.3, bf16[224,1792]{1,0:T(8,128)(2,1)S(1)} %copy-done.4, bf16[128,1792]{1,0:T(8,128)(2,1)S(1)} %copy-done.6, bf16[224,128]{1,0:T(8,128)(2,1)S(1)} %copy-done.7), custom_call_target="tpu_custom_call" | custom-call | flops 4404019200 | bytes 8372224 | tf_op jit(solution)/shard_map/pallas_call | solution.py:347
  86.4 0.1 slice_bitcast_fusion.2
  86.5 0.1 copy.27
  86.6 0.1 copy.34
  86.8 0.2 fusion.20
  87.0 0.2 fusion.21
  87.2 0.2 fusion.22
  87.4 0.2 fusion.23
  87.6 0.2 fusion.24
  87.8 0.2 fusion.28
  88.0 0.1 iota_compare_fusion.2
  88.1 0.5 fusion.43
  88.6 0.2 fusion.42
  88.8 0.1 copy.35
  89.0 1.8 %bitcast_reduce_fusion = (f32[8,48]{1,0:T(8,128)S(1)}, f32[8,48,2048]{2,1,0:T(8,128)S(1)}) fusion(bf16[8,48,224]{2,1,0:T(8,128)(2,1)S(1)} %bitcast.112, bf16[1,224,2048]{2,1,0:T(8,128)(2,1)} %param.19), kind=kOutput, calls=%fused_computation.1 | convolution fusion | flops 353894016 | bytes 4236800 | tf_op jit(solution)/shard_map/rnhe,hep->rnhp/dot_general | solution.py:35
  90.9 0.3 fusion.31
  91.1 0.6 fusion.1
  91.7 0.3 convolution_bitcast_fusion
  92.0 0.7 fusion.7
  92.8 0.7 copy-done.9
  93.5 0.7 fusion.12
  94.2 0.0 all-gather.2.cloned.1.call-done.refs_1_
  94.3 1.5 %copy-done.1 = bf16[3584,224]{1,0:T(8,128)(2,1)S(1)} copy-done((bf16[3584,224]{1,0:T(8,128)(2,1)S(1)}, bf16[3584,224]{1,0:T(8,128)(2,1)}, u32[]{:S(2)}) %copy-start.1) | copy-done | bytes 1605656
  95.8 42.1 %shard_map.128 = bf16[448,384]{1,0:T(8,128)(2,1)S(1)} custom-call(bf16[384,224]{1,0:T(8,128)(2,1)S(1)} %bitcast.109, bf16[3584,224]{1,0:T(8,128)(2,1)S(1)} %copy-done.1), custom_call_target="tpu_custom_call" | custom-call | tf_op jit(solution)/shard_map/pallas_call | solution.py:505
  137.9 0.7 copy.46
  (22 shorter events, 0.1 us)
Async XLA Ops:
  6.5 81.5 %copy-start = (bf16[8,224,512]{2,1,0:T(8,128)(2,1)S(1)}, bf16[8,224,512]{2,1,0:T(8,128)(2,1)}, u32[]{:S(2)}) copy-start(bf16[8,224,512]{2,1,0:T(8,128)(2,1)} %param.21) | copy-start | bytes 5505028
  6.5 87.7 %all-gather.2.cloned.1.call-start = ((), (), s32[]{:S(2)}) async-start(), calls=%async_computation | async-start | bytes 2293760 | tf_op jit(solution)/shard_map/all_gather | solution.py:555
  8.7 1.1 copy-start.2
  9.8 1.1 copy-start.3
  11.0 1.1 copy-start.4
  12.1 1.1 copy-start.5
  13.2 1.0 copy-start.6
  14.2 0.8 copy-start.7
  15.1 71.7 %copy-start.11 = (s32[8,48]{1,0:T(8,128)S(1)}, s32[8,48]{1,0:T(8,128)}, u32[]{:S(2)}) copy-start(s32[8,48]{1,0:T(8,128)} %param.24) | copy-start | bytes 4612
  86.4 1.6 %copy-start.8 = (s32[8]{0:T(128)S(1)}, s32[8]{0:T(128)}, u32[]{:S(2)}) copy-start(s32[8]{0:T(128)} %param.23) | copy-start | bytes 100
  90.8 1.2 copy-start.10
  92.0 1.5 %copy-start.9 = (bf16[8,224,512]{2,1,0:T(8,128)(2,1)S(1)}, bf16[8,224,512]{2,1,0:T(8,128)(2,1)}, u32[]{:S(2)}) copy-start(bf16[8,224,512]{2,1,0:T(8,128)(2,1)} %param.22) | copy-start | bytes 5505028
  94.3 1.5 %copy-start.1 = (bf16[3584,224]{1,0:T(8,128)(2,1)S(1)}, bf16[3584,224]{1,0:T(8,128)(2,1)}, u32[]{:S(2)}) copy-start(bf16[3584,224]{1,0:T(8,128)(2,1)} %all-gather.2.cloned.1.call-done.refs_1_) | copy-start | bytes 4816900
Sparse Core Ops, SparseCore 0:
  8.9 23.8 all-gather.1

commit v2 on v1

--- a/solution.py
+++ b/solution.py
@@ -216,11 +216,15 @@
         both_ways(z, x, p, own(p))
         if p < 2:
             to_x(z, x, p, own(p)).start()
-    rows_buf[pl.ds(pl.multiple_of((2 * z + x) * shard, 16), shard)] = x_ref[...]
+    mine_copy = pltpu.make_async_copy(
+        x_ref, rows_buf.at[pl.ds(pl.multiple_of((2 * z + x) * shard, 16), shard)], w_sem.at[4]
+    )
+    mine_copy.start()
     arrived(z, 1 - x, 2)
     both_ways(z, 1 - x, 2, place(z, 1 - x, 2))
     for load in loads:
         load.wait()
+    mine_copy.wait()
 
     def from_side(oz, below, p, ox):
         @pl.when(jnp.logical_and(oz >= 0, oz < planes))
@@ -347,7 +351,7 @@
     return pl.pallas_call(
         kernel,
         out_shape=jax.ShapeDtypeStruct((3 * query_weight.shape[0], tokens), jnp.bfloat16),
-        in_specs=[vmem, anywhere, anywhere, anywhere, anywhere, vmem],
+        in_specs=[anywhere, anywhere, anywhere, anywhere, anywhere, vmem],
         out_specs=vmem,
         scratch_shapes=[
             pltpu.VMEM((planes * tokens, columns), jnp.bfloat16),
@@ -356,7 +360,7 @@
             pltpu.VMEM((planes // 2, features, tokens), jnp.float32),
             pltpu.VMEM((features, tokens), jnp.bfloat16),
             pltpu.VMEM((features, tokens), jnp.bfloat16),
-            dma((4,)),
+            dma((5,)),
             dma((2 * planes, 3)),
             dma((2 * planes, 3)),
             dma((planes, 3)),
@@ -367,7 +371,7 @@
             dma((1,)),
         ],
         compiler_params=pltpu.CompilerParams(
-            collective_id=0, has_side_effects=True, vmem_limit_bytes=44 * 1024 * 1024
+            collective_id=0, has_side_effects=True, vmem_limit_bytes=60 * 1024 * 1024
         ),
         cost_estimate=pl.CostEstimate(
             flops=2 * planes * tokens * columns * features,
@@ -377,153 +381,160 @@
     )(inputs, query_weight, key_weight, value_weight, adapter_down, adapter_up)
 
 
-def output_kernel(
-    planes,
-    att,
-    weight,
-    out,
-    x_out,
-    x_in,
-    kept,
-    z_out,
-    up_in,
-    down_in,
-    x_send,
-    x_recv,
-    z_send,
-    up_recv,
-    down_recv,
-):
+def gather_kernel(planes, att, out, local_sem, up_send, down_send, x_send, recv):
     z, x = line_position()
-    block = out.shape[0]
+    tokens = att.shape[0]
+    late = tokens // 6 // 16 * 16
+    ranges = ((0, tokens - late), (tokens - late, late))
+    local = pltpu.make_async_copy(att, out.at[2 * z + x], local_sem.at[0])
+    local.start()
     greet_line(planes, z, x, ())
 
-    def partial(oz, ox):
-        rows = weight[pl.ds(pl.multiple_of((2 * oz + ox) * block, 16), block)]
-        return lax.dot_general(rows, att[...], NT, preferred_element_type=jnp.float32)
-
-    def plane_at(k):
-        last = planes - 1
-        low = jnp.where(z == 0, last - k, jnp.where(k == 0, 3, jnp.where(k == 1, 0, 3 - k + 1)))
-        low = jnp.where(jnp.logical_and(z == 1, k == 3), 1, low)
-        m = last - z
-        high = jnp.where(m == 0, last - k, jnp.where(k == 0, 3, jnp.where(k == 1, 0, 3 - k + 1)))
-        high = jnp.where(jnp.logical_and(m == 1, k == 3), 1, high)
-        return jnp.where(z < 2, low, last - high)
-
-    def x_copy(oz):
+    def place(oz, ox, p):
+        first, count = ranges[p]
+        return out.at[2 * oz + ox, pl.ds(first, count)]
+
+    def own(p):
+        first, count = ranges[p]
+        return att.at[pl.ds(first, count)]
+
+    def to_x(oz, ox, p, src):
         return remote(
-            x_out.at[oz], x_in.at[oz], x_send.at[oz], x_recv.at[oz], "gy", 2 * z + 1 - x
-        )
-
-    def up_copy(oz):
+            src, place(oz, ox, p), x_send.at[oz, p], recv.at[2 * oz + ox, p], "gy", 2 * z + 1 - x
+        )
+
+    def to_up(oz, ox, p, src):
         return remote(
-            z_out.at[oz],
-            up_in.at[oz],
-            z_send.at[oz],
-            up_recv.at[oz],
+            src,
+            place(oz, ox, p),
+            up_send.at[2 * oz + ox, p],
+            recv.at[2 * oz + ox, p],
             "gy",
             2 * jnp.minimum(z + 1, planes - 1) + x,
         )
 
-    def down_copy(oz):
+    def to_down(oz, ox, p, src):
         return remote(
-            z_out.at[oz],
-            down_in.at[oz],
-            z_send.at[oz],
-            down_recv.at[oz],
+            src,
+            place(oz, ox, p),
+            down_send.at[2 * oz + ox, p],
+            recv.at[2 * oz + ox, p],
             "gy",
             2 * jnp.maximum(z - 1, 0) + x,
         )
 
-    def cross(k, carry):
-        oz = plane_at(k)
-        x_out[oz] = partial(oz, 1 - x).astype(x_out.dtype)
-        x_copy(oz).start()
+    def arrived(oz, ox, p):
+        ref = place(oz, ox, p)
+        remote(ref, ref, x_send.at[0, 0], recv.at[2 * oz + ox, p], "gy", 2 * z + 1 - x).wait_recv()
+
+    def both_ways(oz, ox, p, src):
+        @pl.when(z < planes - 1)
+        def _():
+            to_up(oz, ox, p, src).start()
+
+        @pl.when(z > 0)
+        def _():
+            to_down(oz, ox, p, src).start()
+
+    to_x(z, x, 1, own(1)).start()
+    for p in (0, 1):
+        both_ways(z, x, p, own(p))
+    to_x(z, x, 0, own(0)).start()
+    arrived(z, 1 - x, 1)
+    both_ways(z, 1 - x, 1, place(z, 1 - x, 1))
+
+    def step(k, carry):
+        for p, same in ((0, True), (1, True), (1, False)):
+            ox = x if same else 1 - x
+            for below in (True, False):
+                oz = z - (k + 1) if below else z + (k + 1)
+
+                @pl.when(jnp.logical_and(oz >= 0, oz < planes))
+                def _():
+                    arrived(oz, ox, p)
+                    src = place(oz, ox, p)
+                    if below:
+
+                        @pl.when(z < planes - 1)
+                        def _():
+                            to_up(oz, ox, p, src).start()
+                    else:
+
+                        @pl.when(z > 0)
+                        def _():
+                            to_down(oz, ox, p, src).start()
+
+                    if p == 0:
+                        to_x(oz, ox, p, src).start()
+
         return carry
 
-    lax.fori_loop(0, planes, cross, 0)
-
-    def keep(k, carry):
-        kept[k] = partial(k, x)
-        return carry
-
-    lax.fori_loop(0, planes, keep, 0)
-
-    def along(k, carry):
-        oz = plane_at(k)
-        x_copy(oz).wait_recv()
-        kept[oz] = kept[oz] + x_in[oz].astype(jnp.float32)
-
-        @pl.when(jnp.logical_and(z > 0, oz >= z))
-        def _():
-            up_copy(oz).wait_recv()
-            kept[oz] = kept[oz] + up_in[oz].astype(jnp.float32)
-
-        @pl.when(jnp.logical_and(z < planes - 1, oz <= z))
-        def _():
-            down_copy(oz).wait_recv()
-            kept[oz] = kept[oz] + down_in[oz].astype(jnp.float32)
-
-        @pl.when(oz > z)
-        def _():
-            z_out[oz] = kept[oz].astype(z_out.dtype)
-            up_copy(oz).start()
-
-        @pl.when(oz < z)
-        def _():
-            z_out[oz] = kept[oz].astype(z_out.dtype)
-            down_copy(oz).start()
-
-        return carry
-
-    lax.fori_loop(0, planes, along, 0)
-    out[...] = kept[z].astype(out.dtype)
-
-    def finish(oz, carry):
-        x_copy(oz).wait_send()
-
-        @pl.when(oz != z)
-        def _():
-            up_copy(oz).wait_send()
-
-        return carry
-
-    lax.fori_loop(0, planes, finish, 0)
-
-
-def project_out(att, weight, planes):
-    tokens = att.shape[0]
-    block = weight.shape[0] // (2 * planes)
+    lax.fori_loop(0, planes - 1, step, 0)
+    local.wait()
+    for oz in range(planes):
+        arrived(oz, 1 - x, 0)
+        to_x(oz, x, 0, place(oz, x, 0)).wait_send()
+        for ox in (0, 1):
+            for p in (0, 1):
+                sent = oz >= 0 if p == 1 else x == ox
+
+                @pl.when(jnp.logical_and(sent, jnp.logical_and(oz <= z, z < planes - 1)))
+                def _():
+                    to_up(oz, ox, p, place(oz, ox, p)).wait_send()
+
+                @pl.when(jnp.logical_and(sent, jnp.logical_and(oz >= z, z > 0)))
+                def _():
+                    to_down(oz, ox, p, place(oz, ox, p)).wait_send()
+
+    to_x(z, x, 1, own(1)).wait_send()
+
+
+def gather_heads(att, planes):
     dma = pltpu.SemaphoreType.DMA
     vmem = pl.BlockSpec(memory_space=pltpu.VMEM)
-    blocks = (planes, block, tokens)
 
     def kernel(*refs):
-        output_kernel(planes, *refs)
+        gather_kernel(planes, *refs)
 
     return pl.pallas_call(
         kernel,
-        out_shape=jax.ShapeDtypeStruct((block, tokens), jnp.bfloat16),
-        in_specs=[vmem, vmem],
+        out_shape=jax.ShapeDtypeStruct((2 * planes,) + att.shape, jnp.bfloat16),
+        in_specs=[vmem],
         out_specs=vmem,
         scratch_shapes=[
-            pltpu.VMEM(blocks, jnp.bfloat16),
-            pltpu.VMEM(blocks, jnp.bfloat16),
-            pltpu.VMEM(blocks, jnp.float32),
-            pltpu.VMEM(blocks, jnp.bfloat16),
-            pltpu.VMEM(blocks, jnp.bfloat16),
-            pltpu.VMEM(blocks, jnp.bfloat16),
-            dma((planes,)),
-            dma((planes,)),
-            dma((planes,)),
-            dma((planes,)),
-            dma((planes,)),
+            dma((1,)),
+            dma((2 * planes, 2)),
+            dma((2 * planes, 2)),
+            dma((planes, 2)),
+            dma((2 * planes, 2)),
         ],
         compiler_params=pltpu.CompilerParams(
-            collective_id=1, has_side_effects=True, vmem_limit_bytes=32 * 1024 * 1024
+            collective_id=1, has_side_effects=True, vmem_limit_bytes=16 * 1024 * 1024
         ),
-    )(att, weight)
+    )(att)
+
+
+def column_block(out_weight):
+    across = lax.axis_size("gx")
+    heads = lax.axis_size("gy")
+    height, width = out_weight.shape
+    cut = out_weight.reshape(across, height // across, 2, width // 2)
+    cut = cut.transpose(0, 2, 1, 3).reshape(heads, height // across, width // 2)
+    h = lax.axis_index("gy")
+    target = 2 * lax.axis_index("gx") + lax.rem(h, 2)
+    got = []
+    for p in range(heads):
+        moves = [
+            (g * heads + k, ((k ^ p) // 2) * heads + 2 * g + (k ^ p) % 2)
+            for g in range(across)
+            for k in range(heads)
+        ]
+        piece = lax.dynamic_index_in_dim(cut, h ^ p, keepdims=False)
+        got.append(lax.ppermute(piece, ("gx", "gy"), moves))
+    mixed = jnp.stack(got)
+    order = jnp.arange(heads, dtype=jnp.int32) ^ target
+    sorted_heads = jnp.take(mixed, order, axis=0)
+    return lax.all_gather(sorted_heads, "gx", axis=1, tiled=True)
 
 
 def per_device(
@@ -552,7 +563,7 @@
     reached = ancestors(parents)
     if lines:
         planes = lax.axis_size("gy") // 2
-        gathered_weight = lax.all_gather(out_weight.T, "gx", axis=0, tiled=True)
+        columns = column_block(out_weight)
         projected = project(
             inputs, query_weight, key_weight, value_weight, adapter_down, adapter_up, planes
         )
@@ -591,7 +602,10 @@
     )
     flattened = attended.reshape(local_rows, head_width)
     if lines:
-        return project_out(flattened, gathered_weight, planes).T
+        everyone = gather_heads(flattened, planes)
+        return jnp.einsum(
+            "hre,hec->rc", everyone, columns, preferred_element_type=jnp.float32
+        ).astype(jnp.bfloat16)
     partial_sums = jnp.dot(
         flattened,
         lax.all_gather(out_weight, "gx", axis=1, tiled=True),

time: 146 us -> 162 us (1.11)
  starting transfers between devices: 0.01 us -> 19.1 us
  Pallas kernels: 113 us -> 98.5 us
  local copies, waits for them, and re-layouts: 11.9 us -> 17.2 us
  matrix products: 5.44 us -> 9.41 us
    ppermute x0 -> x8, starting transfers between devices: none -> 19.1 us  [column_block(): got.append(lax.ppermute(piece, ('gx', 'gy'), moves))]
    pallas_call x1, Pallas kernels: 42.1 us -> 23.1 us  [gather_heads(): pl.pallas_call(kernel, out_shape=jax.ShapeDtypeStruct((2 * planes,) + att...]
    pallas_call x1, Pallas kernels: 71.3 us -> 75.3 us  [project(): pl.pallas_call(kernel, out_shape=jax.ShapeDtypeStruct((3 * query_weight.s...]
    dot_general x0 -> x1, matrix products: none -> 3.41 us  [per_device(): jnp.einsum('hre,hec->rc', everyone, columns, preferred_element_type=jnp.f...]
    unnamed x26 -> x19, local copies, waits for them, and re-layouts: 11.5 us -> 9.61 us
    transpose x2, local copies, waits for them, and re-layouts: 0.2 us -> 1.95 us  [per_device(): queries = projected[:head_width].T]
  transfers between devices with their start and end apart: 1 -> 9, of which waited for: 0 -> 1; matrix products, arithmetic and copies ran while one was open for 5% -> 12% of each run, Pallas kernels for 49% -> 61%
where the time goes in v2:
time: 162 us; the launch traced here: 161 us
  Pallas kernels  98.5 us (61%)
  starting transfers between devices  19.1 us (12%)
  local copies, waits for them, and re-layouts  17.2 us (11%)
  between operations  13.6 us (8%)
  matrix products  9.41 us (6%)
  other arithmetic  1.91 us (1%)
    pallas_call x1, Pallas kernels, project(): pl.pallas_call(kernel, out_shape=jax.ShapeDtypeStruct((3 * query_weight.s...  75.3 us
    pallas_call x1, Pallas kernels, gather_heads(): pl.pallas_call(kernel, out_shape=jax.ShapeDtypeStruct((2 * planes,) + att...  23.1 us
    ppermute x8, starting transfers between devices, column_block(): got.append(lax.ppermute(piece, ('gx', 'gy'), moves))  19.1 us
    unnamed x19, local copies, waits for them, and re-layouts  9.61 us
    dot_general x1, matrix products, per_device(): jnp.einsum('hre,hec->rc', everyone, columns, preferred_element_type=jnp.f...  3.41 us
  transfers between devices with their start and end apart: 9, of which 1 were waited for; matrix products, arithmetic and copies ran while one was open for 12% of the time, Pallas kernels for 61%

profile of v2, /device:TPU:0, one launch (start us, length us, event | category | flops | bytes accessed | tf_op | source)
XLA Modules:
  0.0 161.0 jit_solution(9786173615497651201)
XLA Ops:
  6.5 1.5 reshape.170
  8.2 0.7 dynamic-slice_bitcast_fusion
  8.9 2.1 %collective-permute-start = (bf16[56,448]{1,0:T(8,128)(2,1)}, bf16[56,448]{1,0:T(8,128)(2,1)}, u32[]{:S(2)}, u32[]{:S(2)}) collective-permute-start(bf16[56,448]{1,0:T(8,128)(2,1)} %get-tuple-element.15), channel_id=1, source_target_pairs={{0,0},{1,1},{2,8},{3,9},{4,16},{5,17},{6,24},{7,25},{8,2},{9,3},{1... | collective-permute-start | bytes 150536 | tf_op jit(solution)/shard_map/ppermute | solution.py:533
  11.0 2.9 %collective-permute-start.1 = (bf16[56,448]{1,0:T(8,128)(2,1)}, bf16[56,448]{1,0:T(8,128)(2,1)}, u32[]{:S(2)}, u32[]{:S(2)}) collective-permute-start(bf16[56,448]{1,0:T(8,128)(2,1)} %get-tuple-element.14), channel_id=1, source_target_pairs={{0,1},{1,0},{2,9},{3,8},{4,17},{5,16},{6,25},{7,24},{8,3},{9,2},{1... | collective-permute-start | bytes 150536 | tf_op jit(solution)/shard_map/ppermute | solution.py:533
  13.9 1.0 collective-permute-start.2
  15.2 5.8 %collective-permute-start.4 = (bf16[56,448]{1,0:T(8,128)(2,1)S(1)}, bf16[56,448]{1,0:T(8,128)(2,1)}, u32[]{:S(2)}, u32[]{:S(2)}) collective-permute-start(bf16[56,448]{1,0:T(8,128)(2,1)S(1)} %get-tuple-element.11), channel_id=1, source_target_pairs={{0,16},{1,17},{2,24},{3,25},{4,0},{5,1},{6,8},{7,9},{8,18},{9,19},... | collective-permute-start | bytes 150536 | tf_op jit(solution)/shard_map/ppermute | solution.py:533
  21.1 75.3 %shard_map.127 = bf16[672,384]{1,0:T(8,128)(2,1)} custom-call(bf16[192,1792]{1,0:T(8,128)(2,1)} %refs_0_.1, bf16[224,1792]{1,0:T(8,128)(2,1)} %refs_1_.1, bf16[224,1792]{1,0:T(8,128)(2,1)} %refs_2_.1, bf16[224,1792]{1,0:T(8,128)(2,1)} %refs_3_.1, bf16[128,1792]{1,0:T(8,128)(2,1)} %refs_4_.1, bf16[224,128]{1,0:T(8,128)(2,1)} %refs_5_.1), custom_call_target="tpu_custom_call" | custom-call | flops 4404019200 | bytes 8372224 | tf_op jit(solution)/shard_map/pallas_call | solution.py:351
  96.4 1.8 %slice_bitcast_fusion.2 = (bf16[384,224]{0,1:T(8,128)(2,1)S(1)}, bf16[384,224]{0,1:T(8,128)(2,1)}, bf16[384,224]{0,1:T(8,128)(2,1)S(1)}) fusion(bf16[672,384]{1,0:T(8,128)(2,1)} %shard_map.127), kind=kLoop, calls=%fused_computation.59 | loop fusion | bytes 1032192 | tf_op jit(solution)/shard_map/transpose | solution.py:570
  99.2 0.8 fusion.29
  100.3 0.5 fusion.45
  101.0 3.2 %collective-permute-start.5 = (bf16[56,448]{1,0:T(8,128)(2,1)S(1)}, bf16[56,448]{1,0:T(8,128)(2,1)S(1)}, u32[]{:S(2)}, u32[]{:S(2)}) collective-permute-start(bf16[56,448]{1,0:T(8,128)(2,1)S(1)} %get-tuple-element.10), channel_id=1, source_target_pairs={{0,17},{1,16},{2,25},{3,24},{4,1},{5,0},{6,9},{7,8},{8,19},{9,18},... | collective-permute-start | bytes 150536 | tf_op jit(solution)/shard_map/ppermute | solution.py:533
  104.2 1.4 bitcast_dynamic-update-slice_fusion.7
  105.6 3.6 %collective-permute-start.6 = (bf16[56,448]{1,0:T(8,128)(2,1)S(1)}, bf16[56,448]{1,0:T(8,128)(2,1)S(1)}, u32[]{:S(2)}, u32[]{:S(2)}) collective-permute-start(bf16[56,448]{1,0:T(8,128)(2,1)S(1)} %get-tuple-element.9), channel_id=1, source_target_pairs={{0,24},{1,25},{2,16},{3,17},{4,8},{5,9},{6,0},{7,1},{8,26},{9,27},... | collective-permute-start | bytes 150536 | tf_op jit(solution)/shard_map/ppermute | solution.py:533
  109.2 1.4 bitcast_dynamic-update-slice_fusion.6
  110.8 1.4 bitcast_dynamic-update-slice_fusion.5
  112.2 1.4 bitcast_dynamic-update-slice_fusion.4
  113.6 1.4 bitcast_dynamic-update-slice_fusion.3
  115.1 0.6 bitcast_dynamic-update-slice_fusion.2
  115.7 0.6 bitcast_dynamic-update-slice_fusion.1
  116.3 1.2 collective-permute-done.7
  117.6 0.6 bitcast_dynamic-update-slice_fusion
  118.2 1.6 gather_fusion
  119.8 0.9 broadcast_select_fusion
  120.9 1.1 copy.46
  122.0 1.8 %bitcast_reduce_fusion = (f32[8,48]{1,0:T(8,128)S(1)}, f32[8,48,2048]{2,1,0:T(8,128)S(1)}) fusion(bf16[8,48,224]{2,1,0:T(8,128)(2,1)S(1)} %bitcast.151, bf16[1,224,2048]{2,1,0:T(8,128)(2,1)} %param.19), kind=kOutput, calls=%fused_computation.2 | convolution fusion | flops 353894016 | bytes 4236800 | tf_op jit(solution)/shard_map/rnhe,hep->rnhp/dot_general | solution.py:35
  124.2 0.6 fusion.1
  125.0 0.3 copy-done.4
  125.4 0.7 fusion.8
  126.1 0.8 copy-done.3
  126.9 0.7 fusion.13
  127.6 23.1 %shard_map.128 = bf16[8,384,224]{2,1,0:T(8,128)(2,1)S(1)} custom-call(bf16[384,224]{1,0:T(8,128)(2,1)S(1)} %bitcast.148), custom_call_target="tpu_custom_call" | custom-call | tf_op jit(solution)/shard_map/pallas_call | solution.py:499
  150.8 3.4 %fusion.7 = bf16[384,448]{0,1:T(8,128)(2,1)} fusion(bf16[8,384,224]{2,1,0:T(8,128)(2,1)S(1)} %shard_map.128, bf16[8,224,448]{2,1,0:T(8,128)(2,1)} %all-gather.2.cloned.1.call-done), kind=kOutput, calls=%fused_computation.14 | convolution fusion | flops 616734720 | bytes 3325952 | tf_op jit(solution)/shard_map/hre,hec->rc/dot_general | solution.py:606
  (41 shorter events, 2.6 us)
Async XLA Ops:
  6.5 93.7 %copy-start = (bf16[8,224,512]{2,1,0:T(8,128)(2,1)S(1)}, bf16[8,224,512]{2,1,0:T(8,128)(2,1)}, u32[]{:S(2)}) copy-start(bf16[8,224,512]{2,1,0:T(8,128)(2,1)} %param.21) | copy-start | bytes 5505028
  6.5 144.2 %all-gather.2.cloned.1.call-start = ((), (), s32[]{:S(2)}) async-start(), calls=%async_computation | async-start | bytes 2293760 | tf_op jit(solution)/shard_map/all_gather | solution.py:537
  8.9 92.1 %collective-permute-start = (bf16[56,448]{1,0:T(8,128)(2,1)}, bf16[56,448]{1,0:T(8,128)(2,1)}, u32[]{:S(2)}, u32[]{:S(2)}) collective-permute-start(bf16[56,448]{1,0:T(8,128)(2,1)} %get-tuple-element.15), channel_id=1, source_target_pairs={{0,0},{1,1},{2,8},{3,9},{4,16},{5,17},{6,24},{7,25},{8,2},{9,3},{1... | collective-permute-start | bytes 150536 | tf_op jit(solution)/shard_map/ppermute | solution.py:533
  11.0 94.7 %collective-permute-start.1 = (bf16[56,448]{1,0:T(8,128)(2,1)}, bf16[56,448]{1,0:T(8,128)(2,1)}, u32[]{:S(2)}, u32[]{:S(2)}) collective-permute-start(bf16[56,448]{1,0:T(8,128)(2,1)} %get-tuple-element.14), channel_id=1, source_target_pairs={{0,1},{1,0},{2,9},{3,8},{4,17},{5,16},{6,25},{7,24},{8,3},{9,2},{1... | collective-permute-start | bytes 150536 | tf_op jit(solution)/shard_map/ppermute | solution.py:533
  13.9 96.8 %collective-permute-start.2 = (bf16[56,448]{1,0:T(8,128)(2,1)S(1)}, bf16[56,448]{1,0:T(8,128)(2,1)}, u32[]{:S(2)}, u32[]{:S(2)}) collective-permute-start(bf16[56,448]{1,0:T(8,128)(2,1)S(1)} %get-tuple-element.13), channel_id=1, source_target_pairs={{0,8},{1,9},{2,0},{3,1},{4,24},{5,25},{6,16},{7,17},{8,10},{9,11},... | collective-permute-start | bytes 150536 | tf_op jit(solution)/shard_map/ppermute | solution.py:533
  14.9 97.3 %collective-permute-start.3 = (bf16[56,448]{1,0:T(8,128)(2,1)S(1)}, bf16[56,448]{1,0:T(8,128)(2,1)}, u32[]{:S(2)}, u32[]{:S(2)}) collective-permute-start(bf16[56,448]{1,0:T(8,128)(2,1)S(1)} %get-tuple-element.12), channel_id=1, source_target_pairs={{0,9},{1,8},{2,1},{3,0},{4,25},{5,24},{6,17},{7,16},{8,11},{9,10},... | collective-permute-start | bytes 150536 | tf_op jit(solution)/shard_map/ppermute | solution.py:533
  15.2 98.4 %collective-permute-start.4 = (bf16[56,448]{1,0:T(8,128)(2,1)S(1)}, bf16[56,448]{1,0:T(8,128)(2,1)}, u32[]{:S(2)}, u32[]{:S(2)}) collective-permute-start(bf16[56,448]{1,0:T(8,128)(2,1)S(1)} %get-tuple-element.11), channel_id=1, source_target_pairs={{0,16},{1,17},{2,24},{3,25},{4,0},{5,1},{6,8},{7,9},{8,18},{9,19},... | collective-permute-start | bytes 150536 | tf_op jit(solution)/shard_map/ppermute | solution.py:533
  21.1 77.2 %copy-start.5 = (s32[8,48]{1,0:T(8,128)S(1)}, s32[8,48]{1,0:T(8,128)}, u32[]{:S(2)}) copy-start(s32[8,48]{1,0:T(8,128)} %param.24) | copy-start | bytes 4612
  96.4 3.8 %copy-start.2 = (s32[8]{0:T(128)S(1)}, s32[8]{0:T(128)}, u32[]{:S(2)}) copy-start(s32[8]{0:T(128)} %param.23) | copy-start | bytes 100
  101.0 14.1 %collective-permute-start.5 = (bf16[56,448]{1,0:T(8,128)(2,1)S(1)}, bf16[56,448]{1,0:T(8,128)(2,1)S(1)}, u32[]{:S(2)}, u32[]{:S(2)}) collective-permute-start(bf16[56,448]{1,0:T(8,128)(2,1)S(1)} %get-tuple-element.10), channel_id=1, source_target_pairs={{0,17},{1,16},{2,25},{3,24},{4,1},{5,0},{6,9},{7,8},{8,19},{9,18},... | collective-permute-start | bytes 150536 | tf_op jit(solution)/shard_map/ppermute | solution.py:533
  105.6 10.1 %collective-permute-start.6 = (bf16[56,448]{1,0:T(8,128)(2,1)S(1)}, bf16[56,448]{1,0:T(8,128)(2,1)S(1)}, u32[]{:S(2)}, u32[]{:S(2)}) collective-permute-start(bf16[56,448]{1,0:T(8,128)(2,1)S(1)} %get-tuple-element.9), channel_id=1, source_target_pairs={{0,24},{1,25},{2,16},{3,17},{4,8},{5,9},{6,0},{7,1},{8,26},{9,27},... | collective-permute-start | bytes 150536 | tf_op jit(solution)/shard_map/ppermute | solution.py:533
  110.7 10.0 %copy-start.1 = (pred[8,48,1,48]{1,3,0,2:T(8,128)(4,1)S(1)}, pred[8,48,1,48]{1,3,0,2:T(8,128)(4,1)}, u32[]{:S(2)}) copy-start(pred[8,48,1,48]{1,3,0,2:T(8,128)(4,1)} %fusion.29) | copy-start | bytes 55300
  110.7 6.9 %collective-permute-start.7 = (bf16[56,448]{1,0:T(8,128)(2,1)S(1)}, bf16[56,448]{1,0:T(8,128)(2,1)S(1)}, u32[]{:S(2)}, u32[]{:S(2)}) collective-permute-start(bf16[56,448]{1,0:T(8,128)(2,1)S(1)} %get-tuple-element.8), channel_id=1, source_target_pairs={{0,25},{1,24},{2,17},{3,16},{4,9},{5,8},{6,1},{7,0},{8,27},{9,26},... | collective-permute-start | bytes 150536 | tf_op jit(solution)/shard_map/ppermute | solution.py:533
  124.2 1.2 copy-start.4
  125.4 1.5 copy-start.3
Sparse Core Ops, SparseCore 0:
  120.8 21.1 all-gather.1

commit v3 on v2

--- a/solution.py
+++ b/solution.py
@@ -89,7 +89,7 @@
     return z, x
 
 
-def greet_line(planes, z, x, extra):
+def greet_line(planes, z, x, extra, more=0):
     barrier = pltpu.get_barrier_semaphore()
 
     def signal(axis, index):
@@ -108,7 +108,7 @@
         signal("gy", 2 * (z + 1) + x)
 
     inner = jnp.where(z > 0, 1, 0) + jnp.where(z < planes - 1, 1, 0)
-    pl.semaphore_wait(barrier, 1 + len(extra) + inner)
+    pl.semaphore_wait(barrier, 1 + len(extra) + inner + more)
 
 
 def pieces_of(rows):
@@ -125,7 +125,14 @@
     wv,
     wd,
     up,
+    wo,
     out,
+    cols,
+    halves,
+    o_send,
+    o_recv,
+    spread_send,
+    spread_recv,
     rows_buf,
     weights,
     part,
@@ -163,7 +170,106 @@
         load.start()
         loads.append(load)
         start += count
-    greet_line(planes, z, x, (other_core, other_y))
+
+    gets = core == z - 2 * (z // 2)
+    h = 2 * z + x
+    barrier = pltpu.get_barrier_semaphore()
+    for k in range(2 * planes):
+
+        @pl.when(jnp.logical_and(gets, jnp.logical_or(mine != z, h != k)))
+        def _():
+            pl.semaphore_signal(
+                barrier, inc=1, device_id={"gx": z, "gy": k}, device_id_type=MESH
+            )
+
+    greet_line(planes, z, x, (other_core, other_y), 4 - jnp.where(mine == z, 1, 0))
+    tall = wo.shape[0] // 2
+    across = wo.shape[1] // 2
+
+    def cut_copy(ty, tx, head):
+        return pltpu.make_async_remote_copy(
+            src_ref=halves.at[tx, pl.ds(ty * tall, tall)],
+            dst_ref=cols.at[head, pl.ds(ty * tall, tall)],
+            send_sem=o_send.at[ty, tx],
+            recv_sem=o_recv.at[head],
+            device_id={"gx": 2 * ty + core, "gy": 2 * mine + tx},
+            device_id_type=MESH,
+        )
+
+    def own_cut(ty, tx):
+        return pltpu.make_async_copy(
+            halves.at[tx, pl.ds(ty * tall, tall)],
+            cols.at[h, pl.ds(ty * tall, tall)],
+            o_send.at[ty, tx],
+        )
+
+    def is_own(ty, tx):
+        return jnp.logical_and(mine == z, jnp.logical_and(ty == y, tx == x))
+
+    def spread(slot, part_y, index):
+        rows = cols.at[:, pl.ds(pl.multiple_of(part_y * tall, 16), tall)]
+        return remote(rows, rows, spread_send.at[slot], spread_recv.at[slot], "gx", index)
+
+    def send_cuts():
+        halves[0] = wo[:, :across]
+        halves[1] = wo[:, across:]
+        for ty in (0, 1):
+            for tx in (0, 1):
+
+                @pl.when(is_own(ty, tx))
+                def _():
+                    own_cut(ty, tx).start()
+
+                @pl.when(jnp.logical_not(is_own(ty, tx)))
+                def _():
+                    cut_copy(ty, tx, h).start()
+
+    def spread_first():
+        for ty in (0, 1):
+            for tx in (0, 1):
+
+                @pl.when(is_own(ty, tx))
+                def _():
+                    own_cut(ty, tx).wait()
+
+        @pl.when(gets)
+        def _():
+            for k in range(2 * planes):
+
+                @pl.when(jnp.logical_or(mine != z, h != k))
+                def _():
+                    piece = cols.at[k, pl.ds(pl.multiple_of(y * tall, 16), tall)]
+                    remote(
+                        piece, piece, o_send.at[0, 0], o_recv.at[k], "gx", other_core
+                    ).wait_recv()
+
+            spread(0, y, other_y).start()
+            spread(1, y, other_core).start()
+
+    def spread_second():
+        @pl.when(gets)
+        def _():
+            spread(0, 1 - y, other_y).wait_recv()
+            spread(2, 1 - y, other_core).start()
+
+    def spread_end():
+        @pl.when(gets)
+        def _():
+            spread(0, y, other_y).wait_send()
+            spread(1, y, other_core).wait_send()
+            spread(2, 1 - y, other_core).wait_send()
+
+        @pl.when(jnp.logical_not(gets))
+        def _():
+            spread(1, y, other_core).wait_recv()
+            spread(2, 1 - y, other_core).wait_recv()
+
+        for ty in (0, 1):
+            for tx in (0, 1):
+
+                @pl.when(jnp.logical_not(is_own(ty, tx)))
+                def _():
+                    cut_copy(ty, tx, h).wait_send()
 
     def place(oz, ox, p):
         first, count = ranges[p]
@@ -220,6 +326,7 @@
         x_ref, rows_buf.at[pl.ds(pl.multiple_of((2 * z + x) * shard, 16), shard)], w_sem.at[4]
     )
     mine_copy.start()
+    send_cuts()
     arrived(z, 1 - x, 2)
     both_ways(z, 1 - x, 2, place(z, 1 - x, 2))
     for load in loads:
@@ -287,6 +394,14 @@
         @pl.when(k > 0)
         def _():
             settle(group_at(k - 1))
+
+        @pl.when(k == planes - 2)
+        def _():
+            spread_first()
+
+        @pl.when(k == planes - 1)
+        def _():
+            spread_second()
 
         g = group_at(k)
         for p in (0, 1):
@@ -313,6 +428,7 @@
     out[pl.ds(0, width)] = (total[:width] + extra).astype(jnp.bfloat16)
     out[pl.ds(width, 2 * width)] = total[width : 3 * width].astype(jnp.bfloat16)
 
+    spread_end()
     y_copy().wait_send()
     for half in range(planes // 2):
         core_copy(2 * half + 1 - core).wait_send()
@@ -337,10 +453,13 @@
     to_x(z, x, 2, own(2)).wait_send()
 
 
-def project(inputs, query_weight, key_weight, value_weight, adapter_down, adapter_up, planes):
+def project(
+    inputs, query_weight, key_weight, value_weight, adapter_down, adapter_up, out_weight, planes
+):
     shard, columns = inputs.shape
     features = 3 * query_weight.shape[0] + adapter_down.shape[0]
     tokens = 2 * shard
+    height, half = out_weight.shape[0], out_weight.shape[1] // 2
     dma = pltpu.SemaphoreType.DMA
     vmem = pl.BlockSpec(memory_space=pltpu.VMEM)
     anywhere = pl.BlockSpec(memory_space=pl.ANY)
@@ -350,10 +469,18 @@
 
     return pl.pallas_call(
         kernel,
-        out_shape=jax.ShapeDtypeStruct((3 * query_weight.shape[0], tokens), jnp.bfloat16),
-        in_specs=[anywhere, anywhere, anywhere, anywhere, anywhere, vmem],
-        out_specs=vmem,
+        out_shape=(
+            jax.ShapeDtypeStruct((3 * query_weight.shape[0], tokens), jnp.bfloat16),
+            jax.ShapeDtypeStruct((2 * planes, height, half), jnp.bfloat16),
+        ),
+        in_specs=[anywhere, anywhere, anywhere, anywhere, anywhere, vmem, vmem],
+        out_specs=(vmem, anywhere),
         scratch_shapes=[
+            pltpu.VMEM((2, height, half), jnp.bfloat16),
+            dma((2, 2)),
+            dma((2 * planes,)),
+            dma((3,)),
+            dma((3,)),
             pltpu.VMEM((planes * tokens, columns), jnp.bfloat16),
             pltpu.VMEM((features, columns), jnp.bfloat16),
             pltpu.VMEM((planes, features, tokens), jnp.float32),
@@ -378,7 +505,7 @@
             bytes_accessed=2 * (planes * tokens + features) * columns,
             transcendentals=0,
         ),
-    )(inputs, query_weight, key_weight, value_weight, adapter_down, adapter_up)
+    )(inputs, query_weight, key_weight, value_weight, adapter_down, adapter_up, out_weight)
 
 
 def gather_kernel(planes, att, out, local_sem, up_send, down_send, x_send, recv):
@@ -512,29 +639,6 @@
             collective_id=1, has_side_effects=True, vmem_limit_bytes=16 * 1024 * 1024
         ),
     )(att)
-
-
-def column_block(out_weight):
-    across = lax.axis_size("gx")
-    heads = lax.axis_size("gy")
-    height, width = out_weight.shape
-    cut = out_weight.reshape(across, height // across, 2, width // 2)
-    cut = cut.transpose(0, 2, 1, 3).reshape(heads, height // across, width // 2)
-    h = lax.axis_index("gy")
-    target = 2 * lax.axis_index("gx") + lax.rem(h, 2)
-    got = []
-    for p in range(heads):
-        moves = [
-            (g * heads + k, ((k ^ p) // 2) * heads + 2 * g + (k ^ p) % 2)
-            for g in range(across)
-            for k in range(heads)
-        ]
-        piece = lax.dynamic_index_in_dim(cut, h ^ p, keepdims=False)
-        got.append(lax.ppermute(piece, ("gx", "gy"), moves))
-    mixed = jnp.stack(got)
-    order = jnp.arange(heads, dtype=jnp.int32) ^ target
-    sorted_heads = jnp.take(mixed, order, axis=0)
-    return lax.all_gather(sorted_heads, "gx", axis=1, tiled=True)
 
 
 def per_device(
@@ -563,9 +667,15 @@
     reached = ancestors(parents)
     if lines:
         planes = lax.axis_size("gy") // 2
-        columns = column_block(out_weight)
-        projected = project(
-            inputs, query_weight, key_weight, value_weight, adapter_down, adapter_up, planes
+        projected, columns = project(
+            inputs,
+            query_weight,
+            key_weight,
+            value_weight,
+            adapter_down,
+            adapter_up,
+            out_weight,
+            planes,
         )
         queries = projected[:head_width].T
         new_keys = projected[head_width : 2 * head_width].T

time: 162 us -> 137 us (0.85)
  Pallas kernels: 98.5 us -> 125 us
  starting transfers between devices: 19.1 us -> 0 us
  local copies, waits for them, and re-layouts: 17.2 us -> 1.94 us
  between operations: 13.6 us -> 0.19 us
    pallas_call x1, Pallas kernels: 75.3 us -> 99.8 us  [project(): pl.pallas_call(kernel, out_shape=(jax.ShapeDtypeStruct((3 * query_weight....]
    ppermute x8 -> x0, starting transfers between devices: 19.1 us -> none  [column_block(): got.append(lax.ppermute(piece, ('gx', 'gy'), moves))]
    unnamed x19 -> x12, local copies, waits for them, and re-layouts: 9.61 us -> 0.37 us
    pallas_call x1, Pallas kernels: 23.1 us -> 25 us  [gather_heads(): pl.pallas_call(kernel, out_shape=jax.ShapeDtypeStruct((2 * planes,) + att...]
    dot_general x1, matrix products: 0.71 us -> 2.39 us  [attend(): jnp.einsum('rnhc,rhec->rnhe', w_cache, cache_v, preferred_element_type=jn...]
  transfers between devices with their start and end apart: 9 -> 0, of which waited for: 1 -> 0; matrix products, arithmetic and copies ran while one was open for 12% -> 0% of each run, Pallas kernels for 61% -> 0%
where the time goes in v3:
time: 137 us; the launch traced here: 136 us
  Pallas kernels  125 us (91%)
  matrix products  8.51 us (6%)
  local copies, waits for them, and re-layouts  1.94 us (1%)
    pallas_call x1, Pallas kernels, project(): pl.pallas_call(kernel, out_shape=(jax.ShapeDtypeStruct((3 * query_weight....  99.8 us
    pallas_call x1, Pallas kernels, gather_heads(): pl.pallas_call(kernel, out_shape=jax.ShapeDtypeStruct((2 * planes,) + att...  25 us

profile of v3, /device:TPU:0, one launch (start us, length us, event | category | flops | bytes accessed | tf_op | source)
XLA Modules:
  0.0 136.4 jit_solution(4220047555279588140)
XLA Ops:
  0.0 0.0 copy-start
  0.0 99.8 %shard_map.127 = (bf16[672,384]{1,0:T(8,128)(2,1)}, bf16[8,224,448]{2,1,0:T(8,128)(2,1)}) custom-call(bf16[192,1792]{1,0:T(8,128)(2,1)} %refs_0_.1, bf16[224,1792]{1,0:T(8,128)(2,1)} %refs_1_.1, bf16[224,1792]{1,0:T(8,128)(2,1)} %refs_2_.1, bf16[224,1792]{1,0:T(8,128)(2,1)} %refs_3_.1, bf16[128,1792]{1,0:T(8,128)(2,1)} %refs_4_.1, bf16[224,128]{1,0:T(8,128)(2,1)} %refs_5_.1, ...), custom_call_target="tpu_custom_call" | custom-call | flops 4404019200 | bytes 8372224 | tf_op jit(solution)/shard_map/pallas_call | solution.py:470
  99.8 1.1 slice_bitcast_fusion.2
  101.0 0.0 copy-start.1
  101.0 0.1 copy.28
  101.1 0.1 copy.35
  101.3 0.0 copy-done.4
  101.3 0.2 fusion.21
  101.5 0.2 fusion.22
  101.7 0.2 fusion.23
  101.9 0.2 fusion.24
  102.1 0.2 fusion.25
  102.3 0.2 fusion.29
  102.5 0.2 fusion.43
  102.7 0.0 copy-done.1
  102.7 0.0 copy-start.2
  102.7 0.7 bitcast_reduce_fusion
  103.4 0.0 copy-done.2
  103.4 0.1 iota_compare_fusion.2
  103.5 0.5 fusion.44
  104.0 0.1 fusion.35
  104.1 0.0 copy-start.3
  104.1 0.3 fusion.32
  104.4 0.6 fusion.1
  104.9 0.3 copy-done.3
  105.3 1.4 %fusion.8 = f32[8,48,1,224]{3,1,0,2:T(8,128)} fusion(f32[8,48]{1,0:T(8,128)S(1)} %add_add_fusion, f32[8,48]{1,0:T(8,128)S(1)} %maximum_maximum_fusion, f32[8,48,2048]{2,1,0:T(8,128)S(1)} %get-tuple-element.15, bf16[1,224,2048]{2,1,0:T(8,128)(2,1)S(1)} %copy-done.3), kind=kOutput, calls=%fused_computation.14 | convolution fusion | flops 354680832 | bytes 4410368 | tf_op jit(solution)/shard_map/rnhp,hep->rnhe/dot_general | solution.py:64
  106.7 0.1 copy.36
  106.8 0.3 convolution_bitcast_fusion.1
  107.1 2.4 %fusion.13 = bf16[8,48,1,224]{3,1,0,2:T(8,128)(2,1)S(1)} fusion(f32[8,48,1,224]{3,1,0,2:T(8,128)S(1)} %convolution_bitcast_fusion.1, f32[8,48,1,224]{3,1,0,2:T(8,128)} %fusion.8, bf16[8,224,512]{2,1,0:T(8,128)(2,1)} %param.22, f32[8,48,1,512]{3,1,0,2:T(8,128)S(1)} %get-tuple-element.17, f32[8,48]{1,0:T(8,128)S(1)} %add_add_fusion, ...), kind=kOutput, calls=%fused_computation.19 | convolution fusion | flops 88928256 | bytes 3484672 | tf_op jit(solution)/shard_map/rnhc,rhec->rnhe/dot_general | solution.py:65
  109.5 25.0 %shard_map.128 = bf16[8,384,224]{2,1,0:T(8,128)(2,1)S(1)} custom-call(bf16[384,224]{1,0:T(8,128)(2,1)S(1)} %bitcast.112), custom_call_target="tpu_custom_call" | custom-call | tf_op jit(solution)/shard_map/pallas_call | solution.py:626
  134.5 0.0 copy-done.5
  134.5 1.9 %fusion.7 = bf16[384,448]{0,1:T(8,128)(2,1)} fusion(bf16[8,384,224]{2,1,0:T(8,128)(2,1)S(1)} %shard_map.128, bf16[8,224,448]{2,1,0:T(8,128)(2,1)S(1)} %copy-done.5), kind=kOutput, calls=%fused_computation.13 | convolution fusion | flops 616734720 | bytes 3325952 | tf_op jit(solution)/shard_map/hre,hec->rc/dot_general | solution.py:716
  (6 shorter events, 0.0 us)
Async XLA Ops:
  0.0 103.5 %copy-start = (bf16[8,224,512]{2,1,0:T(8,128)(2,1)S(1)}, bf16[8,224,512]{2,1,0:T(8,128)(2,1)}, u32[]{:S(2)}) copy-start(bf16[8,224,512]{2,1,0:T(8,128)(2,1)} %param.21) | copy-start | bytes 5505028
  0.0 101.3 %copy-start.4 = (s32[8,48]{1,0:T(8,128)S(1)}, s32[8,48]{1,0:T(8,128)}, u32[]{:S(2)}) copy-start(s32[8,48]{1,0:T(8,128)} %param.24) | copy-start | bytes 4612
  101.0 1.7 %copy-start.1 = (bf16[1,224,2048]{2,1,0:T(8,128)(2,1)S(1)}, bf16[1,224,2048]{2,1,0:T(8,128)(2,1)}, u32[]{:S(2)}) copy-start(bf16[1,224,2048]{2,1,0:T(8,128)(2,1)} %param.19) | copy-start | bytes 2752516
  102.7 0.7 copy-start.2
  104.1 1.2 copy-start.3
  107.1 27.4 %copy-start.5 = (bf16[8,224,448]{2,1,0:T(8,128)(2,1)S(1)}, bf16[8,224,448]{2,1,0:T(8,128)(2,1)}, u32[]{:S(2)}) copy-start(bf16[8,224,448]{2,1,0:T(8,128)(2,1)} %get-tuple-element.8) | copy-start | bytes 4816900

commit v4 on v1

--- a/solution.py
+++ b/solution.py
@@ -125,7 +125,11 @@
     wv,
     wd,
     up,
+    wo,
     out,
+    cols,
+    spread_send,
+    spread_recv,
     rows_buf,
     weights,
     part,
@@ -163,7 +167,33 @@
         load.start()
         loads.append(load)
         start += count
+
     greet_line(planes, z, x, (other_core, other_y))
+
+    own_block = pltpu.make_async_copy(wo, cols.at[mine], w_sem.at[5])
+
+    def block_copy(slot, index, target, src):
+        return remote(
+            src, cols.at[index], spread_send.at[slot], spread_recv.at[slot], "gx", target
+        )
+
+    def spread_start():
+        own_block.start()
+        block_copy(0, mine, other_y, wo).start()
+        block_copy(1, mine, other_core, wo).start()
+
+    def spread_second():
+        block_copy(0, other_y, other_y, cols.at[other_y]).wait_recv()
+        block_copy(2, other_y, other_core, cols.at[other_y]).start()
+
+    def spread_end():
+        own_block.wait()
+        block_copy(0, mine, other_y, wo).wait_send()
+        block_copy(1, mine, other_core, wo).wait_send()
+        block_copy(2, other_y, other_core, cols.at[other_y]).wait_send()
+        block_copy(1, other_core, other_core, cols.at[other_core]).wait_recv()
+        cross = 2 * (1 - y) + 1 - core
+        block_copy(2, cross, other_core, cols.at[cross]).wait_recv()
 
     def place(oz, ox, p):
         first, count = ranges[p]
@@ -216,11 +246,16 @@
         both_ways(z, x, p, own(p))
         if p < 2:
             to_x(z, x, p, own(p)).start()
-    rows_buf[pl.ds(pl.multiple_of((2 * z + x) * shard, 16), shard)] = x_ref[...]
+    mine_copy = pltpu.make_async_copy(
+        x_ref, rows_buf.at[pl.ds(pl.multiple_of((2 * z + x) * shard, 16), shard)], w_sem.at[4]
+    )
+    mine_copy.start()
+    spread_start()
     arrived(z, 1 - x, 2)
     both_ways(z, 1 - x, 2, place(z, 1 - x, 2))
     for load in loads:
         load.wait()
+    mine_copy.wait()
 
     def from_side(oz, below, p, ox):
         @pl.when(jnp.logical_and(oz >= 0, oz < planes))
@@ -283,6 +318,10 @@
         @pl.when(k > 0)
         def _():
             settle(group_at(k - 1))
+
+        @pl.when(k == 1)
+        def _():
+            spread_second()
 
         g = group_at(k)
         for p in (0, 1):
@@ -309,6 +348,7 @@
     out[pl.ds(0, width)] = (total[:width] + extra).astype(jnp.bfloat16)
     out[pl.ds(width, 2 * width)] = total[width : 3 * width].astype(jnp.bfloat16)
 
+    spread_end()
     y_copy().wait_send()
     for half in range(planes // 2):
         core_copy(2 * half + 1 - core).wait_send()
@@ -333,7 +373,9 @@
     to_x(z, x, 2, own(2)).wait_send()
 
 
-def project(inputs, query_weight, key_weight, value_weight, adapter_down, adapter_up, planes):
+def project(
+    inputs, query_weight, key_weight, value_weight, adapter_down, adapter_up, out_weight, planes
+):
     shard, columns = inputs.shape
     features = 3 * query_weight.shape[0] + adapter_down.shape[0]
     tokens = 2 * shard
@@ -346,17 +388,22 @@
 
     return pl.pallas_call(
         kernel,
-        out_shape=jax.ShapeDtypeStruct((3 * query_weight.shape[0], tokens), jnp.bfloat16),
-        in_specs=[vmem, anywhere, anywhere, anywhere, anywhere, vmem],
-        out_specs=vmem,
+        out_shape=(
+            jax.ShapeDtypeStruct((3 * query_weight.shape[0], tokens), jnp.bfloat16),
+            jax.ShapeDtypeStruct((planes,) + out_weight.shape, jnp.bfloat16),
+        ),
+        in_specs=[anywhere, anywhere, anywhere, anywhere, anywhere, vmem, anywhere],
+        out_specs=(vmem, anywhere),
         scratch_shapes=[
+            dma((3,)),
+            dma((3,)),
             pltpu.VMEM((planes * tokens, columns), jnp.bfloat16),
             pltpu.VMEM((features, columns), jnp.bfloat16),
             pltpu.VMEM((planes, features, tokens), jnp.float32),
             pltpu.VMEM((planes // 2, features, tokens), jnp.float32),
             pltpu.VMEM((features, tokens), jnp.bfloat16),
             pltpu.VMEM((features, tokens), jnp.bfloat16),
-            dma((4,)),
+            dma((6,)),
             dma((2 * planes, 3)),
             dma((2 * planes, 3)),
             dma((planes, 3)),
@@ -367,14 +414,14 @@
             dma((1,)),
         ],
         compiler_params=pltpu.CompilerParams(
-            collective_id=0, has_side_effects=True, vmem_limit_bytes=44 * 1024 * 1024
+            collective_id=0, has_side_effects=True, vmem_limit_bytes=60 * 1024 * 1024
         ),
         cost_estimate=pl.CostEstimate(
             flops=2 * planes * tokens * columns * features,
             bytes_accessed=2 * (planes * tokens + features) * columns,
             transcendentals=0,
         ),
-    )(inputs, query_weight, key_weight, value_weight, adapter_down, adapter_up)
+    )(inputs, query_weight, key_weight, value_weight, adapter_down, adapter_up, out_weight)
 
 
 def output_kernel(
@@ -398,10 +445,6 @@
     block = out.shape[0]
     greet_line(planes, z, x, ())
 
-    def partial(oz, ox):
-        rows = weight[pl.ds(pl.multiple_of((2 * oz + ox) * block, 16), block)]
-        return lax.dot_general(rows, att[...], NT, preferred_element_type=jnp.float32)
-
     def plane_at(k):
         last = planes - 1
         low = jnp.where(z == 0, last - k, jnp.where(k == 0, 3, jnp.where(k == 1, 0, 3 - k + 1)))
@@ -438,17 +481,16 @@
 
     def cross(k, carry):
         oz = plane_at(k)
-        x_out[oz] = partial(oz, 1 - x).astype(x_out.dtype)
+        both = lax.dot_general(
+            weight[oz], att[...], (((0,), (0,)), ((), ())), preferred_element_type=jnp.float32
+        )
+        low, high = both[:block], both[block:]
+        x_out[oz] = jnp.where(x == 0, high, low).astype(x_out.dtype)
         x_copy(oz).start()
+        kept[oz] = jnp.where(x == 0, low, high)
         return carry
 
     lax.fori_loop(0, planes, cross, 0)
-
-    def keep(k, carry):
-        kept[k] = partial(k, x)
-        return carry
-
-    lax.fori_loop(0, planes, keep, 0)
 
     def along(k, carry):
         oz = plane_at(k)
@@ -493,8 +535,8 @@
 
 
 def project_out(att, weight, planes):
-    tokens = att.shape[0]
-    block = weight.shape[0] // (2 * planes)
+    tokens = att.shape[1]
+    block = weight.shape[2] // 2
     dma = pltpu.SemaphoreType.DMA
     vmem = pl.BlockSpec(memory_space=pltpu.VMEM)
     blocks = (planes, block, tokens)
@@ -552,9 +594,15 @@
     reached = ancestors(parents)
     if lines:
         planes = lax.axis_size("gy") // 2
-        gathered_weight = lax.all_gather(out_weight.T, "gx", axis=0, tiled=True)
-        projected = project(
-            inputs, query_weight, key_weight, value_weight, adapter_down, adapter_up, planes
+        projected, columns = project(
+            inputs,
+            query_weight,
+            key_weight,
+            value_weight,
+            adapter_down,
+            adapter_up,
+            out_weight,
+            planes,
         )
         queries = projected[:head_width].T
         new_keys = projected[head_width : 2 * head_width].T
@@ -591,7 +639,7 @@
     )
     flattened = attended.reshape(local_rows, head_width)
     if lines:
-        return project_out(flattened, gathered_weight, planes).T
+        return project_out(flattened.T, columns, planes).T
     partial_sums = jnp.dot(
         flattened,
         lax.all_gather(out_weight, "gx", axis=1, tiled=True),

time: 146 us -> 133 us (0.911)
  between operations: 13.6 us -> 0.19 us
  local copies, waits for them, and re-layouts: 11.9 us -> 8.29 us
  matrix products: 5.44 us -> 8.44 us
  Pallas kernels: 113 us -> 115 us
    unnamed x26 -> x19, local copies, waits for them, and re-layouts: 11.5 us -> 2.51 us
    dot_general x1, matrix products: 0.72 us -> 3.17 us  [attend(): jnp.einsum('rnhc,rhec->rnhe', w_cache, cache_v, preferred_element_type=jn...]
    transpose x2, local copies, waits for them, and re-layouts: 0.2 us -> 2.05 us  [per_device(): queries = projected[:head_width].T]
    reshape x0 -> x1, local copies, waits for them, and re-layouts: none -> 1.73 us  [per_device(): flattened = attended.reshape(local_rows, head_width)]
    transpose x1, local copies, waits for them, and re-layouts: 0.14 us -> 1.85 us  [per_device(): new_values = projected[2 * head_width:].T]
    pallas_call x1, Pallas kernels: 71.3 us -> 72.9 us  [project(): pl.pallas_call(kernel, out_shape=(jax.ShapeDtypeStruct((3 * query_weight....]
  transfers between devices with their start and end apart: 1 -> 0, of which waited for: 0 -> 0; matrix products, arithmetic and copies ran while one was open for 5% -> 0% of each run, Pallas kernels for 49% -> 0%
where the time goes in v4:
time: 133 us
  Pallas kernels  115 us (86%)
  matrix products  8.44 us (6%)
  local copies, waits for them, and re-layouts  8.29 us (6%)
    pallas_call x1, Pallas kernels, project(): pl.pallas_call(kernel, out_shape=(jax.ShapeDtypeStruct((3 * query_weight....  72.9 us
    pallas_call x1, Pallas kernels, project_out(): pl.pallas_call(kernel, out_shape=jax.ShapeDtypeStruct((block, tokens), jn...  42.2 us
    dot_general x1, matrix products, attend(): jnp.einsum('rnhc,rhec->rnhe', w_cache, cache_v, preferred_element_type=jn...  3.17 us

profile of v4, /device:TPU:0, one launch (start us, length us, event | category | flops | bytes accessed | tf_op | source)
XLA Modules:
  0.0 133.0 jit_solution(392069377202197300)
XLA Ops:
  0.0 0.0 copy-start
  0.0 72.9 %shard_map.127 = (bf16[672,384]{1,0:T(8,128)(2,1)}, bf16[4,224,896]{2,1,0:T(8,128)(2,1)}) custom-call(bf16[192,1792]{1,0:T(8,128)(2,1)} %refs_0_.1, bf16[224,1792]{1,0:T(8,128)(2,1)} %refs_1_.1, bf16[224,1792]{1,0:T(8,128)(2,1)} %refs_2_.1, bf16[224,1792]{1,0:T(8,128)(2,1)} %refs_3_.1, bf16[128,1792]{1,0:T(8,128)(2,1)} %refs_4_.1, bf16[224,128]{1,0:T(8,128)(2,1)} %refs_5_.1, ...), custom_call_target="tpu_custom_call" | custom-call | flops 4404019200 | bytes 8372224 | tf_op jit(solution)/shard_map/pallas_call | solution.py:389
  72.9 0.0 copy-start.4
  72.9 1.9 %slice_bitcast_fusion.2 = (bf16[384,224]{0,1:T(8,128)(2,1)S(1)}, bf16[384,224]{0,1:T(8,128)(2,1)}, bf16[384,224]{0,1:T(8,128)(2,1)S(1)}) fusion(bf16[672,384]{1,0:T(8,128)(2,1)} %get-tuple-element.7), kind=kLoop, calls=%fused_computation.55 | loop fusion | bytes 1032192 | tf_op jit(solution)/shard_map/transpose | solution.py:607
  74.9 0.1 copy.27
  75.0 0.1 copy.34
  75.2 0.0 copy-done.8
  75.2 0.2 fusion.20
  75.4 0.0 copy-start.6
  75.4 0.2 fusion.21
  75.6 0.2 fusion.22
  75.8 0.2 fusion.23
  76.0 0.2 fusion.24
  76.2 0.2 fusion.28
  76.4 0.2 fusion.42
  76.6 0.0 copy-start.5
  76.6 0.0 copy-done.4
  76.6 0.7 bitcast_reduce_fusion
  77.3 0.0 copy-done.6
  77.3 0.1 iota_compare_fusion.2
  77.3 0.5 fusion.43
  78.0 0.8 copy-done.3
  78.8 0.3 fusion.31
  79.0 0.6 fusion.1
  79.6 1.5 %fusion.7 = f32[8,48,1,224]{3,1,0,2:T(8,128)} fusion(f32[8,48]{1,0:T(8,128)S(1)} %add_add_fusion, f32[8,48]{1,0:T(8,128)S(1)} %maximum_maximum_fusion, f32[8,48,2048]{2,1,0:T(8,128)S(1)} %get-tuple-element.15, bf16[1,224,2048]{2,1,0:T(8,128)(2,1)S(1)} %copy-done.7), kind=kOutput, calls=%fused_computation.12 | convolution fusion | flops 354680832 | bytes 4410368 | tf_op jit(solution)/shard_map/rnhp,hep->rnhe/dot_general | solution.py:64
  81.1 1.9 %copy.35 = bf16[384,224]{1,0:T(8,128)(2,1)} copy(bf16[384,224]{0,1:T(8,128)(2,1)} %get-tuple-element.10) | data formatting | bytes 344064 | tf_op jit(solution)/shard_map/transpose | solution.py:609
  82.9 1.3 convolution_bitcast_fusion
  84.2 3.2 %fusion.12 = bf16[8,48,1,224]{3,1,0,2:T(8,128)(2,1)} fusion(f32[8,48,1,224]{3,1,0,2:T(8,128)S(1)} %convolution_bitcast_fusion, f32[8,48,1,224]{3,1,0,2:T(8,128)} %fusion.7, bf16[8,224,512]{2,1,0:T(8,128)(2,1)} %param.22, f32[8,48,1,512]{3,1,0,2:T(8,128)} %copy-done.3, f32[8,48]{1,0:T(8,128)S(1)} %add_add_fusion, f32[8,48]{1,0:T(8,128)S(1)} %maximum_maximum_fusion), kind=kOutput, calls=%fused_computation.17 | convolution fusion | flops 88928256 | bytes 3484672 | tf_op jit(solution)/shard_map/rnhc,rhec->rnhe/dot_general | solution.py:65
  87.4 1.7 %copy.37 = bf16[384,224]{0,1:T(8,128)(2,1)} copy(bf16[384,224]{1,0:T(8,128)(2,1)} %bitcast.114) | data formatting | bytes 344064 | tf_op jit(solution)/shard_map/reshape | solution.py:640
  89.1 0.9 copy-done.2
  90.1 42.2 %shard_map.128 = bf16[448,384]{1,0:T(8,128)(2,1)S(1)} custom-call(bf16[224,384]{1,0:T(8,128)(2,1)S(1)} %bitcast.109, bf16[4,224,896]{2,1,0:T(8,128)(2,1)S(1)} %copy-done.1), custom_call_target="tpu_custom_call" | custom-call | tf_op jit(solution)/shard_map/pallas_call | solution.py:547
  132.3 0.7 copy.46
  (13 shorter events, 0.1 us)
Async XLA Ops:
  0.0 77.3 %copy-start = (bf16[8,224,512]{2,1,0:T(8,128)(2,1)S(1)}, bf16[8,224,512]{2,1,0:T(8,128)(2,1)}, u32[]{:S(2)}) copy-start(bf16[8,224,512]{2,1,0:T(8,128)(2,1)} %param.21) | copy-start | bytes 5505028
  0.0 75.2 %copy-start.8 = (s32[8,48]{1,0:T(8,128)S(1)}, s32[8,48]{1,0:T(8,128)}, u32[]{:S(2)}) copy-start(s32[8,48]{1,0:T(8,128)} %param.24) | copy-start | bytes 4612
  72.9 3.7 %copy-start.4 = (bf16[1,224,2048]{2,1,0:T(8,128)(2,1)S(1)}, bf16[1,224,2048]{2,1,0:T(8,128)(2,1)}, u32[]{:S(2)}) copy-start(bf16[1,224,2048]{2,1,0:T(8,128)(2,1)} %param.19) | copy-start | bytes 2752516
  75.4 1.9 %copy-start.6 = (s32[8]{0:T(128)S(1)}, s32[8]{0:T(128)}, u32[]{:S(2)}) copy-start(s32[8]{0:T(128)} %param.23) | copy-start | bytes 100
  76.6 1.3 copy-start.5
  77.3 2.3 %copy-start.7 = (bf16[1,224,2048]{2,1,0:T(8,128)(2,1)S(1)}, bf16[1,224,2048]{2,1,0:T(8,128)(2,1)}, u32[]{:S(2)}) copy-start(bf16[1,224,2048]{2,1,0:T(8,128)(2,1)} %param.20) | copy-start | bytes 2752516
  77.9 0.9 copy-start.3
  81.1 8.0 %copy-start.1 = (bf16[4,224,896]{2,1,0:T(8,128)(2,1)S(1)}, bf16[4,224,896]{2,1,0:T(8,128)(2,1)}, u32[]{:S(2)}) copy-start(bf16[4,224,896]{2,1,0:T(8,128)(2,1)} %get-tuple-element.8.refs_1_) | copy-start | bytes 4816900
  89.1 0.9 copy-start.2

commit v5 on v4

--- a/solution.py
+++ b/solution.py
@@ -290,23 +290,34 @@
         high = jnp.where(m == 0, k, jnp.where(k == 0, 1, jnp.where(k == 1, 0, k)))
         return jnp.where(z < 2, low, last - high)
 
-    def core_copy(g):
-        return remote(
-            part.at[g], core_in.at[g // 2], c_send.at[g // 2], c_recv.at[g // 2], "gx", other_core
-        )
-
-    def y_copy():
-        return remote(y_out, y_in, y_send.at[0], y_recv.at[0], "gx", other_y)
+    span = weights.shape[0] // 2
+
+    def core_copy(g, i):
+        lines = pl.ds(i * span, span)
+        return remote(
+            part.at[g, lines],
+            core_in.at[g // 2, lines],
+            c_send.at[g // 2, i],
+            c_recv.at[g // 2, i],
+            "gx",
+            other_core,
+        )
+
+    def y_copy(i):
+        lines = pl.ds(i * span, span)
+        return remote(y_out.at[lines], y_in.at[lines], y_send.at[i], y_recv.at[i], "gx", other_y)
 
     def settle(g):
         @pl.when(g - 2 * (g // 2) == core)
         def _():
-            core_copy(g).wait_recv()
-
-            @pl.when(g // 2 != y)
-            def _():
-                y_out[...] = (part[g] + core_in[g // 2]).astype(y_out.dtype)
-                y_copy().start()
+            for i in (0, 1):
+                lines = pl.ds(i * span, span)
+                core_copy(g, i).wait_recv()
+
+                @pl.when(g // 2 != y)
+                def _():
+                    y_out[lines] = (part[g, lines] + core_in[g // 2, lines]).astype(y_out.dtype)
+                    y_copy(i).start()
 
     def step(k, carry):
         distance = k + 1
@@ -326,22 +337,25 @@
         g = group_at(k)
         for p in (0, 1):
             arrived(g, 1 - x, p)
-        part[g] = lax.dot_general(
-            weights[...],
-            rows_buf[pl.ds(pl.multiple_of(g * group_rows, 16), group_rows)],
-            NT,
-            preferred_element_type=jnp.float32,
-        )
-
-        @pl.when(g - 2 * (g // 2) != core)
-        def _():
-            core_copy(g).start()
+        for i in (0, 1):
+            lines = pl.ds(i * span, span)
+            part[g, lines] = lax.dot_general(
+                weights[lines],
+                rows_buf[pl.ds(pl.multiple_of(g * group_rows, 16), group_rows)],
+                NT,
+                preferred_element_type=jnp.float32,
+            )
+
+            @pl.when(g - 2 * (g // 2) != core)
+            def _():
+                core_copy(g, i).start()
 
         return carry
 
     lax.fori_loop(0, planes, step, 0)
     settle(group_at(planes - 1))
-    y_copy().wait_recv()
+    y_copy(0).wait_recv()
+    y_copy(1).wait_recv()
     total = part[mine] + core_in[mine // 2] + y_in[...].astype(jnp.float32)
     middle = total[3 * width :].astype(jnp.bfloat16)
     extra = jnp.dot(up[...], middle, preferred_element_type=jnp.float32)
@@ -349,9 +363,11 @@
     out[pl.ds(width, 2 * width)] = total[width : 3 * width].astype(jnp.bfloat16)
 
     spread_end()
-    y_copy().wait_send()
+    y_copy(0).wait_send()
+    y_copy(1).wait_send()
     for half in range(planes // 2):
-        core_copy(2 * half + 1 - core).wait_send()
+        core_copy(2 * half + 1 - core, 0).wait_send()
+        core_copy(2 * half + 1 - core, 1).wait_send()
     for oz in range(planes):
         for p in (0, 1):
             to_x(oz, x, p, place(oz, x, p)).wait_send()
@@ -408,10 +424,10 @@
             dma((2 * planes, 3)),
             dma((planes, 3)),
             dma((2 * planes, 3)),
-            dma((planes // 2,)),
-            dma((planes // 2,)),
-            dma((1,)),
-            dma((1,)),
+            dma((planes // 2, 2)),
+            dma((planes // 2, 2)),
+            dma((2,)),
+            dma((2,)),
         ],
         compiler_params=pltpu.CompilerParams(
             collective_id=0, has_side_effects=True, vmem_limit_bytes=60 * 1024 * 1024
@@ -482,7 +498,7 @@
     def cross(k, carry):
         oz = plane_at(k)
         both = lax.dot_general(
-            weight[oz], att[...], (((0,), (0,)), ((), ())), preferred_element_type=jnp.float32
+            weight[oz], att[...], (((0,), (1,)), ((), ())), preferred_element_type=jnp.float32
         )
         low, high = both[:block], both[block:]
         x_out[oz] = jnp.where(x == 0, high, low).astype(x_out.dtype)
@@ -535,7 +551,7 @@
 
 
 def project_out(att, weight, planes):
-    tokens = att.shape[1]
+    tokens = att.shape[0]
     block = weight.shape[2] // 2
     dma = pltpu.SemaphoreType.DMA
     vmem = pl.BlockSpec(memory_space=pltpu.VMEM)
@@ -639,7 +655,7 @@
     )
     flattened = attended.reshape(local_rows, head_width)
     if lines:
-        return project_out(flattened.T, columns, planes).T
+        return project_out(flattened, columns, planes).T
     partial_sums = jnp.dot(
         flattened,
         lax.all_gather(out_weight, "gx", axis=1, tiled=True),

time: 133 us -> 127 us (0.955)
  Pallas kernels: 115 us -> 112 us
  local copies, waits for them, and re-layouts: 8.29 us -> 5.64 us
    pallas_call x1, Pallas kernels: 42.2 us -> 39.3 us  [project_out(): pl.pallas_call(kernel, out_shape=jax.ShapeDtypeStruct((block, tokens), jn...]
    reshape x1 -> x0, local copies, waits for them, and re-layouts: 1.73 us -> none  [per_device(): flattened = attended.reshape(local_rows, head_width)]
where the time goes in v5:
time: 127 us
  Pallas kernels  112 us (88%)
  matrix products  7.76 us (6%)
  local copies, waits for them, and re-layouts  5.64 us (4%)
    pallas_call x1, Pallas kernels, project(): pl.pallas_call(kernel, out_shape=(jax.ShapeDtypeStruct((3 * query_weight....  73.1 us
    pallas_call x1, Pallas kernels, project_out(): pl.pallas_call(kernel, out_shape=jax.ShapeDtypeStruct((block, tokens), jn...  39.3 us

profile of v5, /device:TPU:0, one launch (start us, length us, event | category | flops | bytes accessed | tf_op | source)
XLA Modules:
  0.0 127.0 jit_solution(18077117952301321668)
XLA Ops:
  0.0 0.0 copy-start
  0.0 73.1 %shard_map.127 = (bf16[672,384]{1,0:T(8,128)(2,1)}, bf16[4,224,896]{2,1,0:T(8,128)(2,1)}) custom-call(bf16[192,1792]{1,0:T(8,128)(2,1)} %refs_0_.1, bf16[224,1792]{1,0:T(8,128)(2,1)} %refs_1_.1, bf16[224,1792]{1,0:T(8,128)(2,1)} %refs_2_.1, bf16[224,1792]{1,0:T(8,128)(2,1)} %refs_3_.1, bf16[128,1792]{1,0:T(8,128)(2,1)} %refs_4_.1, bf16[224,128]{1,0:T(8,128)(2,1)} %refs_5_.1, ...), custom_call_target="tpu_custom_call" | custom-call | flops 4404019200 | bytes 8372224 | tf_op jit(solution)/shard_map/pallas_call | solution.py:405
  73.2 0.0 copy-start.3
  73.2 1.9 %slice_bitcast_fusion.2 = (bf16[384,224]{0,1:T(8,128)(2,1)S(1)}, bf16[384,224]{0,1:T(8,128)(2,1)}, bf16[384,224]{0,1:T(8,128)(2,1)S(1)}) fusion(bf16[672,384]{1,0:T(8,128)(2,1)} %get-tuple-element.7), kind=kLoop, calls=%fused_computation.55 | loop fusion | bytes 1032192 | tf_op jit(solution)/shard_map/transpose | solution.py:623
  75.1 0.1 copy.26
  75.2 0.1 copy.33
  75.4 0.0 copy-done.7
  75.4 0.2 fusion.20
  75.6 0.0 copy-start.5
  75.6 0.2 fusion.21
  75.8 0.2 fusion.22
  76.0 0.2 fusion.23
  76.2 0.2 fusion.24
  76.4 0.2 fusion.28
  76.6 0.2 fusion.42
  76.8 0.0 copy-start.4
  76.8 0.0 copy-done.3
  76.8 0.7 bitcast_reduce_fusion
  77.5 0.0 copy-done.5
  77.5 0.1 iota_compare_fusion.2
  77.6 0.0 copy-done
  77.6 0.5 fusion.43
  78.1 0.0 copy-done.4
  78.2 0.8 copy-done.2
  79.0 0.3 fusion.31
  79.3 0.6 fusion.1
  79.8 1.5 %fusion.7 = f32[8,48,1,224]{3,1,0,2:T(8,128)} fusion(f32[8,48]{1,0:T(8,128)S(1)} %add_add_fusion, f32[8,48]{1,0:T(8,128)S(1)} %maximum_maximum_fusion, f32[8,48,2048]{2,1,0:T(8,128)S(1)} %get-tuple-element.15, bf16[1,224,2048]{2,1,0:T(8,128)(2,1)S(1)} %copy-done.6), kind=kOutput, calls=%fused_computation.12 | convolution fusion | flops 354680832 | bytes 4410368 | tf_op jit(solution)/shard_map/rnhp,hep->rnhe/dot_general | solution.py:64
  81.3 1.9 %copy.34 = bf16[384,224]{1,0:T(8,128)(2,1)} copy(bf16[384,224]{0,1:T(8,128)(2,1)} %get-tuple-element.10) | data formatting | bytes 344064 | tf_op jit(solution)/shard_map/transpose | solution.py:625
  83.2 1.3 %convolution_bitcast_fusion = f32[8,48,1,224]{3,1,0,2:T(8,128)S(1)} fusion(bf16[8,48,224]{2,1,0:T(8,128)(2,1)} %bitcast.113, f32[8,48,1,48]{1,3,0,2:T(8,128)} %copy-done.4, f32[8,48]{1,0:T(8,128)S(1)} %add_add_fusion, f32[8,48]{1,0:T(8,128)S(1)} %maximum_maximum_fusion), kind=kOutput, calls=%fused_computation.13 | convolution fusion | flops 8312832 | bytes 592896 | tf_op jit(solution)/shard_map/rnhm,rmhe->rnhe/dot_general | solution.py:68
  84.4 2.5 %fusion.12 = bf16[8,48,1,224]{3,1,0,2:T(8,128)(2,1)S(1)} fusion(f32[8,48,1,224]{3,1,0,2:T(8,128)S(1)} %convolution_bitcast_fusion, f32[8,48,1,224]{3,1,0,2:T(8,128)} %fusion.7, bf16[8,224,512]{2,1,0:T(8,128)(2,1)} %param.22, f32[8,48,1,512]{3,1,0,2:T(8,128)} %copy-done.2, f32[8,48]{1,0:T(8,128)S(1)} %add_add_fusion, f32[8,48]{1,0:T(8,128)S(1)} %maximum_maximum_fusion), kind=kOutput, calls=%fused_computation.17 | convolution fusion | flops 88928256 | bytes 3484672 | tf_op jit(solution)/shard_map/rnhc,rhec->rnhe/dot_general | solution.py:65
  87.0 39.3 %shard_map.128 = bf16[448,384]{1,0:T(8,128)(2,1)S(1)} custom-call(bf16[384,224]{1,0:T(8,128)(2,1)S(1)} %bitcast.108, bf16[4,224,896]{2,1,0:T(8,128)(2,1)S(1)} %copy-done.1), custom_call_target="tpu_custom_call" | custom-call | tf_op jit(solution)/shard_map/pallas_call | solution.py:563
  126.2 0.7 copy.44
  (10 shorter events, 0.1 us)
Async XLA Ops:
  0.0 77.6 %copy-start = (bf16[8,224,512]{2,1,0:T(8,128)(2,1)S(1)}, bf16[8,224,512]{2,1,0:T(8,128)(2,1)}, u32[]{:S(2)}) copy-start(bf16[8,224,512]{2,1,0:T(8,128)(2,1)} %param.21) | copy-start | bytes 5505028
  0.0 75.4 %copy-start.7 = (s32[8,48]{1,0:T(8,128)S(1)}, s32[8,48]{1,0:T(8,128)}, u32[]{:S(2)}) copy-start(s32[8,48]{1,0:T(8,128)} %param.24) | copy-start | bytes 4612
  73.2 3.7 %copy-start.3 = (bf16[1,224,2048]{2,1,0:T(8,128)(2,1)S(1)}, bf16[1,224,2048]{2,1,0:T(8,128)(2,1)}, u32[]{:S(2)}) copy-start(bf16[1,224,2048]{2,1,0:T(8,128)(2,1)} %param.19) | copy-start | bytes 2752516
  75.6 1.9 %copy-start.5 = (s32[8]{0:T(128)S(1)}, s32[8]{0:T(128)}, u32[]{:S(2)}) copy-start(s32[8]{0:T(128)} %param.23) | copy-start | bytes 100
  76.8 1.3 %copy-start.4 = (f32[8,48,1,48]{1,3,0,2:T(8,128)}, f32[8,48,1,48]{1,3,0,2:T(8,128)S(1)}, u32[]{:S(2)}) copy-start(f32[8,48,1,48]{1,3,0,2:T(8,128)S(1)} %get-tuple-element.13) | copy-start | bytes 221188
  77.6 2.3 %copy-start.6 = (bf16[1,224,2048]{2,1,0:T(8,128)(2,1)S(1)}, bf16[1,224,2048]{2,1,0:T(8,128)(2,1)}, u32[]{:S(2)}) copy-start(bf16[1,224,2048]{2,1,0:T(8,128)(2,1)} %param.20) | copy-start | bytes 2752516
  78.1 0.9 copy-start.2
  81.3 5.6 %copy-start.1 = (bf16[4,224,896]{2,1,0:T(8,128)(2,1)S(1)}, bf16[4,224,896]{2,1,0:T(8,128)(2,1)}, u32[]{:S(2)}) copy-start(bf16[4,224,896]{2,1,0:T(8,128)(2,1)} %get-tuple-element.8.refs_1_) | copy-start | bytes 4816900

commit v6 on v5

--- a/solution.py
+++ b/solution.py
@@ -359,8 +359,9 @@
     total = part[mine] + core_in[mine // 2] + y_in[...].astype(jnp.float32)
     middle = total[3 * width :].astype(jnp.bfloat16)
     extra = jnp.dot(up[...], middle, preferred_element_type=jnp.float32)
-    out[pl.ds(0, width)] = (total[:width] + extra).astype(jnp.bfloat16)
-    out[pl.ds(width, 2 * width)] = total[width : 3 * width].astype(jnp.bfloat16)
+    out[0] = (total[:width] + extra).T.astype(jnp.bfloat16)
+    out[1] = total[width : 2 * width].T.astype(jnp.bfloat16)
+    out[2] = total[2 * width : 3 * width].T.astype(jnp.bfloat16)
 
     spread_end()
     y_copy(0).wait_send()
@@ -405,7 +406,7 @@
     return pl.pallas_call(
         kernel,
         out_shape=(
-            jax.ShapeDtypeStruct((3 * query_weight.shape[0], tokens), jnp.bfloat16),
+            jax.ShapeDtypeStruct((3, tokens, query_weight.shape[0]), jnp.bfloat16),
             jax.ShapeDtypeStruct((planes,) + out_weight.shape, jnp.bfloat16),
         ),
         in_specs=[anywhere, anywhere, anywhere, anywhere, anywhere, vmem, anywhere],
@@ -620,9 +621,9 @@
             out_weight,
             planes,
         )
-        queries = projected[:head_width].T
-        new_keys = projected[head_width : 2 * head_width].T
-        new_values = projected[2 * head_width :].T
+        queries = projected[0]
+        new_keys = projected[1]
+        new_values = projected[2]
     else:
         all_rows = lax.all_gather(inputs, "gy", axis=0, tiled=True)
         mixture = lax.psum_scatter(

time: 127 us -> 122 us (0.961)
  local copies, waits for them, and re-layouts: 5.64 us -> 2.81 us
  matrix products: 7.76 us -> 5.05 us
    transpose x4 -> x0, local copies, waits for them, and re-layouts: 4.05 us -> none  [the longest x2 2.05 us: per_device(): queries = projected[:head_width].T]
    dot_general x1, matrix products: 2.49 us -> 0.72 us  [attend(): jnp.einsum('rnhc,rhec->rnhe', w_cache, cache_v, preferred_element_type=jn...]
where the time goes in v6:
time: 122 us
  Pallas kernels  112 us (92%)
  matrix products  5.05 us (4%)
  local copies, waits for them, and re-layouts  2.81 us (2%)
  other arithmetic  1.75 us (1%)
    pallas_call x1, Pallas kernels, project(): pl.pallas_call(kernel, out_shape=(jax.ShapeDtypeStruct((3, tokens, query_...  73 us
    pallas_call x1, Pallas kernels, project_out(): pl.pallas_call(kernel, out_shape=jax.ShapeDtypeStruct((block, tokens), jn...  39.2 us

profile of v6, /device:TPU:0, one launch (start us, length us, event | category | flops | bytes accessed | tf_op | source)
XLA Modules:
  0.0 122.0 jit_solution(16140625688149299922)
XLA Ops:
  0.0 0.0 copy-start
  0.0 0.9 iota_compare_fusion.2
  0.9 1.0 fusion.20
  1.9 0.2 fusion.21
  2.1 0.2 fusion.22
  2.3 0.2 fusion.23
  2.5 0.2 fusion.24
  2.7 0.2 fusion.28
  2.9 73.0 %shard_map.127 = (bf16[3,384,224]{2,1,0:T(8,128)(2,1)}, bf16[4,224,896]{2,1,0:T(8,128)(2,1)}) custom-call(bf16[192,1792]{1,0:T(8,128)(2,1)} %refs_0_.1, bf16[224,1792]{1,0:T(8,128)(2,1)} %refs_1_.1, bf16[224,1792]{1,0:T(8,128)(2,1)} %refs_2_.1, bf16[224,1792]{1,0:T(8,128)(2,1)} %refs_3_.1, bf16[128,1792]{1,0:T(8,128)(2,1)} %refs_4_.1, ...), custom_call_target="tpu_custom_call" | custom-call | flops 4404019200 | bytes 8372224 | tf_op jit(solution)/shard_map/pallas_call | solution.py:406
  75.9 0.0 copy-start.2
  75.9 1.2 %fusion.42 = (bf16[1,384,224]{2,1,0:T(8,128)(2,1)S(1)}, bf16[1,384,224]{2,1,0:T(8,128)(2,1)S(1)}, bf16[1,384,224]{2,1,0:T(8,128)(2,1)S(1)}) fusion(bf16[3,384,224]{2,1,0:T(8,128)(2,1)} %get-tuple-element.7), kind=kLoop, calls=%fused_computation.64 | loop fusion | bytes 1032192 | tf_op jit(solution)/shard_map/slice | solution.py:624
  77.1 0.2 fusion.43
  77.3 0.0 copy-done
  77.4 0.5 fusion.44
  77.9 0.0 copy-done.2
  77.9 0.7 bitcast_reduce_fusion
  78.6 0.0 copy-start.4
  78.6 0.3 fusion.31
  78.9 0.6 fusion.1
  79.5 0.3 copy-done.4
  79.7 0.0 copy-start.3
  79.7 0.7 fusion.7
  80.5 0.0 copy-start.1
  80.5 0.3 convolution_bitcast_fusion
  80.8 0.5 copy-done.3
  81.2 0.7 fusion.12
  82.0 0.1 copy-done.1
  82.1 39.2 %shard_map.128 = bf16[448,384]{1,0:T(8,128)(2,1)S(1)} custom-call(bf16[384,224]{1,0:T(8,128)(2,1)S(1)} %bitcast.102, bf16[4,224,896]{2,1,0:T(8,128)(2,1)S(1)} %copy-done.1), custom_call_target="tpu_custom_call" | custom-call | tf_op jit(solution)/shard_map/pallas_call | solution.py:564
  121.2 0.7 copy.29
  (4 shorter events, 0.1 us)
Async XLA Ops:
  0.0 77.3 %copy-start = (bf16[8,224,512]{2,1,0:T(8,128)(2,1)S(1)}, bf16[8,224,512]{2,1,0:T(8,128)(2,1)}, u32[]{:S(2)}) copy-start(bf16[8,224,512]{2,1,0:T(8,128)(2,1)} %param.21) | copy-start | bytes 5505028
  75.9 2.0 %copy-start.2 = (bf16[1,224,2048]{2,1,0:T(8,128)(2,1)S(1)}, bf16[1,224,2048]{2,1,0:T(8,128)(2,1)}, u32[]{:S(2)}) copy-start(bf16[1,224,2048]{2,1,0:T(8,128)(2,1)} %param.19) | copy-start | bytes 2752516
  78.6 1.2 copy-start.4
  79.7 1.5 %copy-start.3 = (bf16[8,224,512]{2,1,0:T(8,128)(2,1)S(1)}, bf16[8,224,512]{2,1,0:T(8,128)(2,1)}, u32[]{:S(2)}) copy-start(bf16[8,224,512]{2,1,0:T(8,128)(2,1)} %param.22) | copy-start | bytes 5505028
  80.5 1.6 %copy-start.1 = (bf16[4,224,896]{2,1,0:T(8,128)(2,1)S(1)}, bf16[4,224,896]{2,1,0:T(8,128)(2,1)}, u32[]{:S(2)}) copy-start(bf16[4,224,896]{2,1,0:T(8,128)(2,1)} %get-tuple-element.8.refs_1_) | copy-start | bytes 4816900
